TPU v7x, 256 devices: a whole 4x4x8 slice. The times are simulated.
256 devices in a mesh: face: 8 (over x, core), patch: 32 (over y, z).
Axes of the slice: x: 4, y: 4, z: 8, core: 2. Of those that a mesh axis runs over, the one named last changes fastest.
Arguments:
- nodes: float32 [131072, 512], P(('face', 'patch')), may hold values from -6 to 6
- edges: bfloat16 [1048576, 512], P(('face', 'patch')), may hold values from -6 to 6
- sender: int32 [1048576], P(('face', 'patch')), may hold values from 0 to 8959, as said below
- receiver: int32 [1048576], P(('face', 'patch')), may hold values from 0 to 512, as said below
- send_rows: int32 [1024, 64], P(('face', 'patch')), may hold values from 0 to 511
- w_sender: bfloat16 [512, 512], replicated, may hold values from -0.25 to 0.25
- w_receiver: bfloat16 [512, 512], replicated, may hold values from -0.25 to 0.25
- w_edge: bfloat16 [512, 512], replicated, may hold values from -0.25 to 0.25
- bias_edge1: float32 [512], replicated, may hold values from -3 to 3
- w_edge2: bfloat16 [512, 512], replicated, may hold values from -0.25 to 0.25
- bias_edge2: float32 [512], replicated, may hold values from -3 to 3
- gain_edge: float32 [512], replicated, may hold values from 0.1 to 1.9
- shift_edge: float32 [512], replicated, may hold values from -3 to 3
- w_node_self: bfloat16 [512, 512], replicated, may hold values from -0.25 to 0.25
- w_node_aggr: bfloat16 [512, 512], replicated, may hold values from -0.25 to 0.25
- bias_node1: float32 [512], replicated, may hold values from -3 to 3
- w_node2: bfloat16 [512, 512], replicated, may hold values from -0.25 to 0.25
- bias_node2: float32 [512], replicated, may hold values from -3 to 3
- gain_node: float32 [512], replicated, may hold values from 0.1 to 1.9
- shift_node: float32 [512], replicated, may hold values from -3 to 3
Outputs:
- new_nodes: float32 [131072, 512], P(('face', 'patch'))
- new_edges: bfloat16 [1048576, 512], P(('face', 'patch'))
Inputs may be any that keep to these rules, and one draw needn't show every extreme that they name: `sender`: rows below 512 are the device's own nodes, the next 256 its halo, the rest the coarse rows. `receiver`: within each device's slots the receivers never fall; empty slots come last and carry 512.
All inputs are finite; a program needn't handle non-finite values.
Results may differ from a plain program's by a relative error of at most 0.0055.
Values may be sent and summed in bfloat16 or wider, within the bound.
No kernel may reach another device: no remote copies, remote signals or barrier semaphores. Data moves between devices by JAX's collectives and lax.ppermute only.
A program may use at most 128 MiB of HBM per device.

v0:
```python
import functools

import numpy as np
import jax
import jax.numpy as jnp
from jax import lax
from jax.experimental import pallas as pl
from jax.experimental.pallas import tpu as pltpu
from jax.sharding import Mesh, PartitionSpec as P

AXES = ("x", "core", "y", "z")
SIZES = (4, 2, 4, 8)
NODE = 512
HALO = 64
NEAR = NODE + 4 * HALO
COARSE_DEV = 32
D = 512
EDGE = 4096
TILE = 1024
TILES = EDGE // TILE
BLOCK = 256
SLOTS = 768
BLOCKS = 18
LATE = 2
WINDOW = 240
SUB = 512
F32 = jnp.float32
BF16 = jnp.bfloat16

STAGES = (
    (((0, 0, 4),) * 2,),
    (((2, 0, 0), (0, 2, 0)), ((0, 2, 0), (2, 0, 0)), ((2, 2, 0),) * 2),
    (((1, 1, 1), (-1, -1, -1)), ((-1, -1, -1), (1, 1, 1)), ((0, 0, 2), (0, 0, -2))),
)
LAST = (((1, 0, 0), (-1, 0, 0)), ((0, 1, 0), (0, -1, 0)), ((0, 0, 1), (0, 0, -1)))


def places():
    own = np.zeros((2, 128), np.int32)
    for core in range(2):
        held = [(0, 0, 0)]
        for stage in STAGES + (LAST,):
            held = [
                ((a[0] + o[0]) % 4, (a[1] + o[1]) % 4, (a[2] + o[2]) % 8)
                for o in [(0, 0, 0)] + [pair[core] for pair in stage]
                for a in held
            ]
        assert len(set(held)) == 128
        for block, (x, y, z) in enumerate(held):
            own[core, x * 32 + y * 8 + z] = block
    return np.stack([np.stack([own[c] if c == k else 128 + own[k] for k in range(2)]) for c in range(2)])


PLACES = places()


def device(x, c, y, z):
    return ((x % 4) * 2 + c % 2) * 32 + (y % 4) * 8 + z % 8


def receive(block, source):
    spots = [(x, c, y, z) for x in range(4) for c in range(2) for y in range(4) for z in range(8)]
    return lax.ppermute(block, AXES, [(device(*source(*spot)), device(*spot)) for spot in spots])


def from_chip(block, pair):
    return receive(block, lambda x, c, y, z: (x + pair[c][0], c, y + pair[c][1], z + pair[c][2]))


def other_core(block):
    return receive(block, lambda x, c, y, z: (x, 1 - c, y, z))


def shift_patch(block, step):
    def source(x, c, y, z):
        j = (y * 8 + z - step) % 32
        return x, c, j // 8, j % 8

    return receive(block, source)


def next_chip(block):
    return receive(block, lambda x, c, y, z: (x - 1 + 2 * c, 1 - c, y, z))


def dot(a, b):
    return jnp.dot(a, b, preferred_element_type=F32)


def dot_first(a, b):
    return lax.dot_general(a, b, (((0,), (0,)), ((), ())), preferred_element_type=F32)


def dot_last(a, b):
    return lax.dot_general(a, b, (((1,), (1,)), ((), ())), preferred_element_type=F32)


def silu(v):
    half = 0.5 * v
    return half + half * jnp.tanh(half)


def layer_norm(v, gain, shift):
    center = v - jnp.mean(v, axis=-1, keepdims=True)
    spread = jnp.mean(center * center, axis=-1, keepdims=True)
    return center * lax.rsqrt(spread + 1e-05) * gain + shift


def iota(shape, dim):
    return lax.broadcasted_iota(jnp.int32, shape, dim)


def pick_kernel(spot_ref, nodes_ref, rows_ref, own_ref, *out_refs):
    own = nodes_ref[...].astype(BF16)
    own_ref[...] = own
    core = spot_ref[3]
    for row, out_ref in zip((0, 1, 3 - core, 2 + core), out_refs):
        hot = (iota((NODE, HALO), 0) == rows_ref[pl.ds(row, 1), :]).astype(BF16)
        out_ref[...] = dot_first(hot, own).astype(BF16)


def compact_kernel(
    spot_ref, snd_ref, rcv_ref, edges_ref, own_ref, w_sender_ref, w_receiver_ref, w_edge_ref, b1_ref, place_ref,
    slot_ref, info_ref, code_out_ref, rcv_out_ref, ts_ref, tr_ref, far_edges_ref, far_pre_ref,
    upper, far_edges, far_meta, far_pre, count, sems,
):
    ts_ref[...] = dot(own_ref[...], w_sender_ref[...]).astype(BF16)
    tr_ref[...] = dot(own_ref[...], w_receiver_ref[...]).astype(BF16)
    upper[...] = (iota((TILE, TILE), 0) < iota((TILE, TILE), 1)).astype(BF16)
    rcv_out_ref[...] = jnp.full_like(rcv_out_ref, NODE)
    count[0] = 0

    def tile(t, carry):
        compact_tile(
            t, spot_ref, snd_ref, rcv_ref, edges_ref, slot_ref, info_ref, upper, far_edges, far_meta, count,
        )
        return carry

    lax.fori_loop(0, TILES, tile, 0)
    total = count[0]
    info_ref[TILES] = total
    blocks = (total + BLOCK - 1) // BLOCK

    def copies(b):
        rows = pl.ds(pl.multiple_of(b * BLOCK, BLOCK), BLOCK)
        return (
            pltpu.make_async_copy(far_edges.at[rows], far_edges_ref.at[rows], sems.at[b, 0]),
            pltpu.make_async_copy(far_pre.at[rows], far_pre_ref.at[rows], sems.at[b, 1]),
        )

    def push(b, carry):
        info = far_meta[b].astype(jnp.int32)
        spots = (iota((256, BLOCK), 0) == info[0:1]).astype(BF16)
        block = dot(place_ref[...], spots)[0:1].astype(jnp.int32)
        code_out_ref[b] = block * 32 + info[1:2]
        live = iota((1, BLOCK), 1) + b * BLOCK < total
        rcv_b = jnp.where(live, info[2:3] * 128 + info[3:4], NODE)
        rcv_out_ref[b] = rcv_b
        rows = pl.ds(pl.multiple_of(b * BLOCK, BLOCK), BLOCK)
        hot = (iota((NODE, BLOCK), 0) == jnp.minimum(rcv_b, NODE - 1)).astype(BF16)
        far_pre[rows] = dot(far_edges[rows], w_edge_ref[...]) + dot_first(hot, tr_ref[...]) + b1_ref[...]
        for copy in copies(b):
            copy.start()
        return carry

    lax.fori_loop(0, blocks, push, 0)

    def settle(b, carry):
        for copy in copies(b):
            copy.wait()
        return carry

    lax.fori_loop(0, blocks, settle, 0)


def compact_tile(t, spot_ref, snd_ref, rcv_ref, edges_ref, slot_ref, info_ref, upper, far_edges, far_meta, count):
    rcv = rcv_ref[t]
    snd = snd_ref[t]
    far = snd >= NEAR
    q = jnp.maximum(snd - NEAR, 0)
    p = q >> 5
    dx = ((p >> 6) - spot_ref[0]) & 3
    dy = ((p >> 3) - spot_ref[1]) & 3
    dz = (p - spot_ref[2]) & 7
    place = (((p >> 5) & 1) << 7) | (dx << 5) | (dy << 3) | dz
    far_f = far.astype(F32)
    base = count[0]
    before = dot(jnp.broadcast_to(far_f, (8, TILE)).astype(BF16), upper[...])[0:1].astype(jnp.int32)
    number = jnp.sum(far_f).astype(jnp.int32)
    slot = jnp.where(far, base + before, -1)
    slot_ref[t] = slot
    info_ref[t] = base
    count[0] = base + number
    first = base // BLOCK
    last = jnp.where(number > 0, (base + number - 1) // BLOCK + 1, first)
    zero = jnp.zeros_like(rcv)
    meta = jnp.concatenate([place, q & 31, rcv >> 7, rcv & 127, zero, zero, zero, zero], axis=0)
    meta = meta.astype(F32).astype(BF16)

    def gather(b, carry):
        hot = (iota((BLOCK, TILE), 0) + b * BLOCK == slot).astype(BF16)
        rows = pl.ds(pl.multiple_of(b * BLOCK, BLOCK), BLOCK)
        fresh = b * BLOCK >= base
        far_edges[rows] = jnp.where(fresh, 0.0, far_edges[rows]) + dot(hot, edges_ref[pl.ds(pl.multiple_of(t * TILE, TILE), TILE)]).astype(BF16)
        far_meta[b] = jnp.where(fresh, 0.0, far_meta[b]) + dot_last(meta, hot)
        return carry

    lax.fori_loop(first, last, gather, 0)


def near_kernel(begin, end, pieces, *refs):
    (
        snd_ref, rcv_ref, edges_ref, tr_ref,
        w_edge_ref, b1_ref, w2_ref, b2_ref, gain_ref, shift_ref,
    ) = refs[:10]
    window, snd_c, rcv_c, updates = refs[-4:]
    if begin == 0:
        spot_ref, own_ts_ref, h0_ref, h1_ref, h2_ref, h3_ref, w_sender_ref = refs[10:17]
        new_edges_ref, agg_ref, ts_ref = refs[17:20]
        w_sender = w_sender_ref[...]
        ts_ref[:NODE] = own_ts_ref[...]
        core = spot_ref[3]
        for k, h_ref in zip((0, 1, 2 + core, 3 - core), (h0_ref, h1_ref, h2_ref, h3_ref)):
            there = pl.ds(pl.multiple_of(NODE + k * HALO, HALO), HALO)
            ts_ref[there] = dot(h_ref[...], w_sender).astype(BF16)
        agg_ref[...] = jnp.zeros_like(agg_ref)
    else:
        ts_ref = refs[10]
        ready = refs[13:13 + pieces]
        new_edges_ref, agg_ref = refs[13 + pieces:15 + pieces]
        if pieces:
            table, sems = refs[15 + pieces:17 + pieces]
        copies = [
            pltpu.make_async_copy(piece, table.at[k * 1024:(k + 1) * 1024], sems.at[k])
            for k, piece in enumerate(ready)
        ]
        for copy in copies:
            copy.start()
    window[WINDOW:] = tr_ref[NODE - 16:]

    def edge_rows(at, col, hots, tables):
        edges = edges_ref[at]
        pre = dot(edges, w_edge_ref[...]) + b1_ref[...]
        for hot, part in zip(hots, tables):
            pre = pre + dot(hot, part)
        hidden = silu(pre).astype(BF16)
        update = layer_norm(dot(hidden, w2_ref[...]) + b2_ref[...], gain_ref[...], shift_ref[...])
        new_edges_ref[at] = jnp.where(col >= 0, edges.astype(F32) + update, 0.0).astype(BF16)
        return update.astype(BF16)

    def columns(*rows):
        both = jnp.concatenate(list(rows) * 4, axis=0)
        cols = jnp.transpose(both.astype(F32), (1, 0)).astype(jnp.int32)
        return cols[:, 0:1], cols[:, 1:2]

    def step(i, carry):
        snd = snd_ref[i]
        rcv = rcv_ref[i]
        far = snd >= NEAR
        live = rcv < NODE
        low = jnp.min(rcv)
        high = jnp.max(jnp.where(live, rcv, -1))
        start = pl.multiple_of(jnp.minimum(low // 16 * 16, NODE - WINDOW), 16)
        narrow = high - start < WINDOW
        snd_n = jnp.where(far, -1, snd)

        @pl.when(narrow)
        def _():
            window[:WINDOW] = tr_ref[pl.ds(start, WINDOW)]
            snd_v, rcv_v = columns(snd_n, jnp.where(live, rcv - start, WINDOW + 15))
            parts = []
            for k in range(0, TILE, SUB):
                col = snd_v[k:k + SUB]
                hot_s = (iota((SUB, NEAR), 1) == col).astype(BF16)
                hot_r = (iota((SUB, 256), 1) == rcv_v[k:k + SUB]).astype(BF16)
                at = pl.ds(pl.multiple_of(i * TILE + k, SUB), SUB)
                parts.append(edge_rows(at, col, [hot_s, hot_r], [ts_ref[...], window[...]]))
            hot_n = (iota((WINDOW, TILE), 0) == jnp.where(far, -1, rcv - start)).astype(BF16)
            agg_ref[pl.ds(start, WINDOW)] += dot(hot_n, jnp.concatenate(parts, axis=0))

        @pl.when(jnp.logical_not(narrow))
        def _():
            snd_v, rcv_v = columns(snd_n, jnp.minimum(rcv, NODE - 1))
            snd_c[...] = snd_v
            rcv_c[...] = rcv_v

            def some(j, c):
                at = pl.ds(pl.multiple_of(j * 128, 128), 128)
                col = snd_c[at]
                hot_s = (iota((128, NEAR), 1) == col).astype(BF16)
                hot_r = (iota((128, NODE), 1) == rcv_c[at]).astype(BF16)
                there = pl.ds(pl.multiple_of(i * TILE + j * 128, 128), 128)
                updates[at] = edge_rows(there, col, [hot_s, hot_r], [ts_ref[...], tr_ref[...]])
                return c

            lax.fori_loop(0, TILE // 128, some, 0)

            def sums(j, c):
                at = pl.ds(pl.multiple_of(j * 128, 128), 128)
                hot_n = (iota((128, TILE), 0) + j * 128 == jnp.where(far, -1, rcv)).astype(BF16)
                agg_ref[at] += dot(hot_n, updates[...])
                return c

            lax.fori_loop(0, NODE // 128, sums, 0)

        return carry

    lax.fori_loop(begin, end, step, 0)
    if begin and pieces:
        for copy in copies:
            copy.wait()


def far_kernel(info_ref, code_ref, *refs):
    late = refs[1:1 + LATE]
    (
        _, far_edges_ref, far_pre_ref, agg_ref, slot_ref, rcv_ref, nodes_ref,
        w_sender, w2, w_self, w_aggr, wn2,
        b2_ref, gain_ref, shift_ref, bn1_ref, bn2_ref, gain_n_ref, shift_n_ref,
        new_nodes_ref, new_edges_ref, table, near,
        rows_buf, edges_buf, pre_buf, new_far, agg, sems, near_sems, row_sems,
    ) = refs[1 + LATE:]
    copies = [
        pltpu.make_async_copy(piece, table.at[(8 - LATE + k) * 1024:(9 - LATE + k) * 1024], sems.at[k])
        for k, piece in enumerate(late)
    ]

    def block_copies(b):
        rows = pl.ds(pl.multiple_of(b * SLOTS, SLOTS), SLOTS)
        return (
            pltpu.make_async_copy(far_edges_ref.at[rows], edges_buf, row_sems.at[0]),
            pltpu.make_async_copy(far_pre_ref.at[rows], pre_buf, row_sems.at[1]),
        )

    total = info_ref[TILES]
    for copy in copies:
        copy.start()

    @pl.when(total > 0)
    def _():
        for copy in block_copies(0):
            copy.start()

    agg[...] = agg_ref[...]
    inner_self = dot(nodes_ref[...].astype(BF16), w_self[...]) + bn1_ref[...]
    for copy in copies:
        copy.wait()

    def block(b, carry):
        @pl.when(b > 0)
        def _():
            for copy in block_copies(b):
                copy.start()

        count = jnp.minimum(SLOTS, (total - b * SLOTS + 15) // 16 * 16)

        row = b * (SLOTS // BLOCK)

        def gather(i, c):
            for k in range(16):
                slot = i * 16 + k
                code = code_ref[row + (slot >> 8), 0, slot & 255]
                rows_buf[pl.ds(pl.multiple_of(slot * 4, 4), 4)] = table[code].astype(F32)
            return c

        lax.fori_loop(0, count // 16, gather, 0)
        for copy in block_copies(b):
            copy.wait()
        for k in range(SLOTS // BLOCK):
            here = slice(k * BLOCK, (k + 1) * BLOCK)
            first = b * SLOTS + k * BLOCK
            valid = iota((BLOCK, 1), 0) + first < total
            sent = jnp.concatenate(
                [rows_buf[pl.ds(k * BLOCK * 4 + c, BLOCK, stride=4)] for c in range(4)], axis=1
            ).astype(BF16)
            pre = pre_buf[here] + dot(sent, w_sender[...])
            hidden = silu(pre).astype(BF16)
            update = layer_norm(dot(hidden, w2[...]) + b2_ref[...], gain_ref[...], shift_ref[...])
            update = jnp.where(valid, update, 0.0)
            new = jnp.where(valid, edges_buf[here].astype(F32) + update, 0.0)
            new_far[pl.ds(pl.multiple_of(first, BLOCK), BLOCK)] = new.astype(BF16)
            hot = (iota((NODE, BLOCK), 0) == rcv_ref[b * (SLOTS // BLOCK) + k]).astype(BF16)
            agg[...] += dot(hot, update.astype(BF16))
        return carry

    lax.fori_loop(0, (total + SLOTS - 1) // SLOTS, block, 0)

    def store(t):
        rows = pl.ds(pl.multiple_of(t * TILE, TILE), TILE)
        return pltpu.make_async_copy(near.at[rows], new_edges_ref.at[rows], near_sems.at[t])

    def tile(t, carry):
        base = info_ref[t]
        end = info_ref[t + 1]
        first = base // BLOCK
        last = jnp.where(end > base, (end - 1) // BLOCK + 1, first)
        rows = pl.ds(pl.multiple_of(t * TILE, TILE), TILE)
        slots = jnp.concatenate([slot_ref[t]] * 8, axis=0).astype(F32)
        slots = jnp.transpose(slots, (1, 0)).astype(jnp.int32)[:, 0:1]

        def scatter(b, c):
            hot = (iota((TILE, BLOCK), 1) + b * BLOCK == slots).astype(BF16)
            there = pl.ds(pl.multiple_of(b * BLOCK, BLOCK), BLOCK)
            near[rows] = near[rows] + dot(hot, new_far[there]).astype(BF16)
            return c

        lax.fori_loop(first, last, scatter, 0)
        store(t).start()
        return carry

    lax.fori_loop(0, TILES, tile, 0)
    inner = silu(inner_self + dot(agg[...].astype(BF16), w_aggr[...])).astype(BF16)
    out = layer_norm(dot(inner, wn2[...]) + bn2_ref[...], gain_n_ref[...], shift_n_ref[...])
    new_nodes_ref[...] = nodes_ref[...] + out
    for t in range(TILES):
        store(t).wait()


def full(shape):
    return pl.BlockSpec(shape, lambda *_: (0,) * len(shape))


ANY = pl.BlockSpec(memory_space=pl.ANY)
SMEM = pl.BlockSpec(memory_space=pltpu.SMEM)
VMEM = pl.BlockSpec(memory_space=pltpu.VMEM)
HBM = pl.BlockSpec(memory_space=pltpu.HBM)
ROW = pl.BlockSpec((1, 1, TILE), lambda t: (t, 0, 0))
EDGES = pl.BlockSpec((TILE, D), lambda t: (t, 0))
SQUARE = full((D, D))
VECTOR = full((1, D))


def kept(dims, kind):
    return pltpu.VMEM(dims, kind)


def keep(array):
    return pltpu.with_memory_space_constraint(array, pltpu.VMEM)


def far_away(array):
    return pltpu.with_memory_space_constraint(array, pltpu.HBM)


def shape(dims, kind):
    return jax.ShapeDtypeStruct(dims, kind)


def load_kernel(*refs):
    count = (len(refs) - 1) // 2
    copies = [pltpu.make_async_copy(refs[k], refs[count + k], refs[-1].at[k]) for k in range(count)]
    for copy in copies:
        copy.start()
    for copy in copies:
        copy.wait()


def load(*arrays):
    count = len(arrays)
    return pl.pallas_call(
        load_kernel,
        in_specs=[HBM] * count,
        out_specs=[VMEM] * count,
        out_shape=[kept(array.shape, array.dtype) for array in arrays],
        scratch_shapes=[pltpu.SemaphoreType.DMA((count,))],
        compiler_params=pltpu.CompilerParams(vmem_limit_bytes=16 << 20),
        cost_estimate=pl.CostEstimate(flops=0, bytes_accessed=16 << 20, transcendentals=0),
    )(*(far_away(array) for array in arrays))


def pick(spot, nodes, send_rows):
    return pl.pallas_call(
        pick_kernel,
        in_specs=[SMEM, VMEM, VMEM],
        out_specs=[VMEM] * 5,
        out_shape=(kept((NODE, D), BF16),) + (shape((HALO, D), BF16),) * 4,
        compiler_params=pltpu.CompilerParams(vmem_limit_bytes=16 << 20),
        cost_estimate=pl.CostEstimate(flops=2 * NODE * D * 256, bytes_accessed=2 << 20, transcendentals=0),
    )(spot, nodes, send_rows)


def compact(*args):
    rows = BLOCKS * BLOCK
    return pl.pallas_call(
        compact_kernel,
        in_specs=[SMEM] + [VMEM] * (len(args) - 1),
        out_specs=[VMEM, SMEM, VMEM, VMEM, VMEM, VMEM, HBM, HBM],
        out_shape=(
            kept((TILES, 1, TILE), jnp.int32), shape((16,), jnp.int32),
            shape((BLOCKS, 1, BLOCK), jnp.int32), kept((BLOCKS, 1, BLOCK), jnp.int32),
            kept((NODE, D), BF16), kept((NODE, D), BF16),
            pltpu.HBM((rows, D), BF16), pltpu.HBM((rows, D), F32),
        ),
        scratch_shapes=[
            pltpu.VMEM((TILE, TILE), BF16), pltpu.VMEM((rows, D), BF16),
            pltpu.VMEM((BLOCKS, 8, BLOCK), F32), pltpu.VMEM((rows, D), F32),
            pltpu.SMEM((1,), jnp.int32), pltpu.SemaphoreType.DMA((BLOCKS, 2)),
        ],
        compiler_params=pltpu.CompilerParams(vmem_limit_bytes=30 << 20),
        cost_estimate=pl.CostEstimate(flops=4 << 30, bytes_accessed=8 << 20, transcendentals=0),
    )(*args)


def near(begin, end, pieces, *args):
    outs = [kept((EDGE, D), BF16), kept((NODE, D), F32)]
    scratch = [
        pltpu.VMEM((256, D), BF16), pltpu.VMEM((TILE, 1), jnp.int32), pltpu.VMEM((TILE, 1), jnp.int32),
        pltpu.VMEM((TILE, D), BF16),
    ]
    if begin == 0:
        outs = outs + [kept((NEAR, D), BF16)]
    if pieces:
        outs = outs + [kept((8192, 4, 128), BF16)]
        scratch = [pltpu.SemaphoreType.DMA((pieces,))] + scratch
    return pl.pallas_call(
        functools.partial(near_kernel, begin, end, pieces),
        in_specs=[SMEM if k == 10 and begin == 0 else VMEM for k in range(len(args))],
        out_specs=[VMEM] * len(outs),
        out_shape=outs,
        scratch_shapes=scratch,
        input_output_aliases={11: 0, 12: 1} if begin else {},
        compiler_params=pltpu.CompilerParams(vmem_limit_bytes=16 << 20),
        cost_estimate=pl.CostEstimate(flops=(end - begin) << 31, bytes_accessed=(end - begin) << 21, transcendentals=0),
    )(*args)


def far(*args):
    return pl.pallas_call(
        far_kernel,
        in_specs=[SMEM] * 2 + [VMEM] + [ANY] * LATE + [VMEM] + [HBM] * 2 + [VMEM] * (len(args) - 6 - LATE),
        out_specs=[VMEM, ANY, VMEM, VMEM],
        out_shape=(shape((NODE, D), F32), shape((EDGE, D), BF16), kept((8192, 4, 128), BF16), kept((EDGE, D), BF16)),
        input_output_aliases={2: 2, 3 + LATE: 3},
        scratch_shapes=[
            pltpu.VMEM((4 * SLOTS, 128), F32),
            pltpu.VMEM((SLOTS, D), BF16), pltpu.VMEM((SLOTS, D), F32), pltpu.VMEM((BLOCKS * BLOCK, D), BF16),
            pltpu.VMEM((NODE, D), F32),
            pltpu.SemaphoreType.DMA((LATE,)), pltpu.SemaphoreType.DMA((TILES,)), pltpu.SemaphoreType.DMA((2,)),
        ],
        compiler_params=pltpu.CompilerParams(vmem_limit_bytes=24 << 20),
        cost_estimate=pl.CostEstimate(flops=4 << 30, bytes_accessed=24 << 20, transcendentals=1 << 20),
    )(*args)


def body(
    nodes, edges, sender, receiver, send_rows,
    w_sender, w_receiver, w_edge, bias_edge1, w_edge2, bias_edge2, gain_edge, shift_edge,
    w_node_self, w_node_aggr, bias_node1, w_node2, bias_node2, gain_node, shift_node,
):
    row = lambda v: v.reshape(1, D)
    tiles = lambda v: v.reshape(TILES, 1, TILE)
    after = lambda v, *first: lax.optimization_barrier((v,) + first)[0]
    x, c, y, z = (lax.axis_index(a) for a in AXES)
    spot = jnp.stack([x, y, z, c]).astype(jnp.int32)
    held = nodes[:COARSE_DEV].astype(BF16).reshape(COARSE_DEV, 4, 128)
    nodes = keep(nodes)
    own, *out = pick(spot, nodes, send_rows)
    own = keep(own)
    tables = jnp.asarray(np.repeat(PLACES.reshape(2, 1, 256), 8, axis=1), BF16)
    place = jnp.where(c == 0, tables[0], tables[1])

    def grow(held, stage, *first):
        got = [from_chip(held, pair) for pair in stage]
        return jnp.concatenate([after(held, *first)] + got, axis=0)

    across = [next_chip(out[2]), other_core(out[3])]
    held = after(grow(held, STAGES[0]), *across)
    halo = [shift_patch(after(out[0], held), 1), shift_patch(after(out[1], held), -1)] + across
    names = load(
        after(edges, held), tiles(sender), tiles(receiver), w_sender, w_edge, w_edge2, w_receiver,
        w_node_self, w_node_aggr, w_node2,
        row(bias_edge1), row(bias_edge2), row(gain_edge), row(shift_edge),
        row(bias_node1), row(bias_node2), row(gain_node), row(shift_node),
    )
    (
        edges, snd, rcv, w_sender, w_edge, w_edge2, w_receiver, w_node_self, w_node_aggr, w_node2,
        bias_edge1, *vectors,
    ) = (keep(v) for v in names)
    edge_vectors, node_vectors = vectors[:3], vectors[3:]

    def edge_part(begin, end, pieces, *extra):
        outs = near(begin, end, pieces, snd, rcv, edges, tr, w_edge, bias_edge1, w_edge2, *edge_vectors, *extra)
        return [keep(v) for v in outs]

    held = after(grow(held, STAGES[1]), edges, *halo)
    slot, info, far_code, far_rcv, own_ts, tr, far_edges, far_pre = compact(
        spot, snd, rcv, edges, keep(after(own, held)), w_sender, w_receiver, w_edge, bias_edge1, place,
    )
    slot, far_rcv, own_ts, tr = (keep(v) for v in (slot, far_rcv, own_ts, tr))
    held = grow(held, STAGES[2], tr)
    last = [from_chip(held, pair) for pair in LAST]
    done, agg, ts = edge_part(0, 2, 0, spot, keep(after(own_ts, held)), *halo, w_sender)
    first = [other_core(held), other_core(after(last[0], agg))]
    done, agg = edge_part(2, 3, 0, ts, done, agg)
    second = [other_core(after(piece, agg)) for piece in last[1:]]
    early = [held, *last, *first]
    done, agg, table = edge_part(3, 4, 6, ts, done, agg, *early)
    new_nodes, new_edges, _, _ = far(
        info, far_code, table, *second, done,
        far_away(far_edges), far_away(far_pre), agg, slot, far_rcv, nodes,
        w_sender, w_edge2, w_node_self, w_node_aggr, w_node2, *edge_vectors, *node_vectors,
    )
    return new_nodes, new_edges


def solution(mesh):
    grid = Mesh(mesh.devices.reshape(SIZES), AXES)
    split = P(AXES, None)
    return jax.shard_map(
        body,
        mesh=grid,
        in_specs=(split, split, P(AXES), P(AXES), split) + (P(),) * 15,
        out_specs=(split, split),
        check_vma=False,
    )
```

profile of v0, /device:TPU:1, one launch (start us, length us, event | category | flops | bytes accessed | tf_op | source)
XLA Modules:
  0.0 88.4 jit_solution(6868695288050346680)
XLA Ops:
  0.6 0.8 slice.15
  1.5 7.8 %collective-permute-start = (bf16[32,4,128]{2,1,0:T(4,128)(2,1)S(1)}, bf16[32,4,128]{2,1,0:T(4,128)(2,1)S(1)}, u32[]{:S(2)}, u32[]{:S(2)}) collective-permute-start(bf16[32,4,128]{2,1,0:T(4,128)(2,1)S(1)} %reshape.39), channel_id=1, source_target_pairs={{4,0},{5,1},{6,2},{7,3},{0,4},{1,5},{2,6},{3,7},{12,8},{13,9},{14,... | collective-permute-start | bytes 98312 | tf_op jit(solution)/shard_map/ppermute | solution.py:63
  9.3 0.1 pad_add_fusion.spot_ref.refs_10_
  9.4 0.0 copy-start
  9.4 1.2 %copy-done = f32[512,512]{1,0:T(8,128)S(1)} copy-done((f32[512,512]{1,0:T(8,128)S(1)}, f32[512,512]{1,0:T(8,128)}, u32[]{:S(2)}) %copy-start) | copy-done | bytes 1048600
  10.6 0.0 copy-start.2
  10.6 0.7 copy-done.2
  11.3 1.0 %shard_map.212 = (bf16[512,512]{1,0:T(8,128)(2,1)S(1)}, bf16[64,512]{1,0:T(8,128)(2,1)S(1)}, bf16[64,512]{1,0:T(8,128)(2,1)S(1)}, bf16[64,512]{1,0:T(8,128)(2,1)S(1)}, bf16[64,512]{1,0:T(8,128)(2,1)S(1)}) custom-call(s32[4]{0:T(128)S(1)} %pad_add_fusion.spot_ref.refs_10_, f32[512,512]{1,0:T(8,128)S(1)} %copy-done, s32[4,64]{1,0:T(4,128)S(1)} %copy-done.2), custom_call_target="tpu_custom_call" | custom-call | flops 134217728 | bytes 2097152 | tf_op jit(solution)/shard_map/pallas_call | solution.py:472
  12.4 2.1 %collective-permute-start.1 = (bf16[64,512]{1,0:T(8,128)(2,1)S(1)}, bf16[64,512]{1,0:T(8,128)(2,1)S(1)}, u32[]{:S(2)}, u32[]{:S(2)}) collective-permute-start(bf16[64,512]{1,0:T(8,128)(2,1)S(1)} %get-tuple-element.54), channel_id=1, source_target_pairs={{224,0},{225,1},{226,2},{227,3},{228,4},{229,5},{230,6},{231,7},{2... | collective-permute-start | bytes 196616 | tf_op jit(solution)/shard_map/ppermute | solution.py:63
  14.5 0.8 collective-permute-start.2
  15.3 0.0 collective-permute-done
  15.4 1.1 %collective-permute-done.1.refs_14_ = bf16[64,512]{1,0:T(8,128)(2,1)S(1)} collective-permute-done((bf16[64,512]{1,0:T(8,128)(2,1)S(1)}, bf16[64,512]{1,0:T(8,128)(2,1)S(1)}, u32[]{:S(2)}, u32[]{:S(2)}) %collective-permute-start.1) | collective-permute-done | bytes 65568 | tf_op jit(solution)/shard_map/ppermute | solution.py:63
  16.5 0.0 collective-permute-done.2.refs_15_
  16.5 5.4 %collective-permute-start.5 = (bf16[64,4,128]{2,1,0:T(4,128)(2,1)S(1)}, bf16[64,4,128]{2,1,0:T(4,128)(2,1)S(1)}, u32[]{:S(2)}, u32[]{:S(2)}) collective-permute-start(bf16[64,4,128]{2,1,0:T(4,128)(2,1)S(1)} %pad_maximum_fusion.1), channel_id=1, source_target_pairs={{144,0},{145,1},{146,2},{147,3},{148,4},{149,5},{150,6},{151,7},{1... | collective-permute-start | bytes 196616 | tf_op jit(solution)/shard_map/ppermute | solution.py:63
  21.8 0.2 collective-permute-start.4
  22.1 0.1 collective-permute-start.3
  22.1 0.7 select_bitcast_fusion.place_ref
  22.8 0.7 collective-permute-start.6
  23.6 4.0 %collective-permute-start.7 = (bf16[64,512]{1,0:T(8,128)(2,1)S(1)}, bf16[64,512]{1,0:T(8,128)(2,1)S(1)}, u32[]{:S(2)}, u32[]{:S(2)}) collective-permute-start(bf16[64,512]{1,0:T(8,128)(2,1)S(1)} %get-tuple-element.65), channel_id=1, source_target_pairs={{1,0},{2,1},{3,2},{4,3},{5,4},{6,5},{7,6},{8,7},{9,8},{10,9},{11,1... | collective-permute-start | bytes 196616 | tf_op jit(solution)/shard_map/ppermute | solution.py:63
  27.6 3.4 %shard_map.213 = (bf16[4096,512]{1,0:T(8,128)(2,1)S(1)}, s32[4,1,1024]{2,1,0:T(1,128)S(1)}, s32[4,1,1024]{2,1,0:T(1,128)S(1)}, bf16[512,512]{1,0:T(8,128)(2,1)S(...) custom-call(bf16[4096,512]{1,0:T(8,128)(2,1)} %refs_0_, ...), custom_call_target="tpu_custom_call" | custom-call | bytes 16777216 | tf_op jit(solution)/shard_map/pallas_call | solution.py:460
  31.0 0.0 collective-permute-done.5
  31.0 0.0 collective-permute-done.4
  31.1 0.0 collective-permute-done.3
  31.1 0.2 pad_maximum_fusion
  31.3 0.0 collective-permute-done.6.refs_12_
  31.3 0.0 collective-permute-done.7.refs_13_
  31.3 0.1 collective-permute-start.10
  31.4 5.7 %collective-permute-start.9 = (bf16[256,4,128]{2,1,0:T(4,128)(2,1)S(1)}, bf16[256,4,128]{2,1,0:T(4,128)(2,1)S(1)}, u32[]{:S(2)}, u32[]{:S(2)}) collective-permute-start(bf16[256,4,128]{2,1,0:T(4,128)(2,1)S(1)} %pad_maximum_fusion), channel_id=1, source_target_pairs={{223,0},{216,1},{217,2},{218,3},{219,4},{220,5},{221,6},{222,7},{1... | collective-permute-start | bytes 786440 | tf_op jit(solution)/shard_map/ppermute | solution.py:63
  37.1 0.0 collective-permute-start.8
  37.1 9.4 %shard_map.214 = (s32[4,1,1024]{2,1,0:T(1,128)S(1)}, s32[16]{0:T(128)S(1)}, s32[18,1,256]{2,1,0:T(1,128)S(1)}, s32[18,1,256]{2,1,0:T(1,128)S(1)}, bf16[512,512]{...) custom-call(s32[4]{0:T(128)S(1)} %pad_add_fusion.spot_ref.refs_10_, ...), custom_call_target="tpu_custom_call" | custom-call | flops 4294967296 | bytes 8388608 | tf_op jit(solution)/shard_map/pallas_call | solution.py:484
  46.6 0.1 constant_dynamic-update-slice_fusion.3
  46.7 3.1 %collective-permute-done.8 = bf16[256,4,128]{2,1,0:T(4,128)(2,1)S(1)} collective-permute-done((bf16[256,4,128]{2,1,0:T(4,128)(2,1)S(1)}, bf16[256,4,128]{2,1,0:T(4,128)(2,1)S(1)}, u32[]{:S(2)}, u32[]{:S(2)}) %collective-permute-start.8) | collective-permute-done | bytes 262176 | tf_op jit(solution)/shard_map/ppermute | solution.py:63
  49.7 0.1 constant_dynamic-update-slice_fusion.2
  49.9 0.0 collective-permute-done.9
  49.9 0.1 constant_dynamic-update-slice_fusion.1
  50.0 0.0 collective-permute-done.10
  50.0 0.1 constant_dynamic-update-slice_fusion.refs_13_
  50.1 0.1 collective-permute-start.11
  50.2 0.1 collective-permute-start.13
  50.3 0.3 collective-permute-start.12
  50.6 6.3 %collective-permute-start.14 = (bf16[1024,4,128]{2,1,0:T(4,128)(2,1)S(1)}, bf16[1024,4,128]{2,1,0:T(4,128)(2,1)S(1)}, u32[]{:S(2)}, u32[]{:S(2)}) collective-permute-start(bf16[1024,4,128]{2,1,0:T(4,128)(2,1)S(1)} %constant_dynamic-update-slice_fusion.refs_13_), channel_id=1, source_target_pairs={{32,0},{33,1},{34,2},{35,3},{36,4},{37,5},{38,6},{39,7},{40,8},{41... | collective-permute-start | bytes 3145736 | tf_op jit(solution)/shard_map/ppermute | solution.py:63
  56.8 8.2 %shard_map.215 = (bf16[4096,512]{1,0:T(8,128)(2,1)S(1)}, f32[512,512]{1,0:T(8,128)S(1)}, bf16[768,512]{1,0:T(8,128)(2,1)S(1)}) custom-call(s32[4,1,1024]{2,1,0:T(1,128)S(1)} %get-tuple-element.58.snd_ref.refs_0_, s32[4,1,1024]{2,1,0:T(1,128)S(1)} %get-tuple-element.59.rcv_ref.refs_1_, bf16[4096,512]{1,0:T(8,128)(2,1)S(1)} %get-tuple-element.60.edges_ref.refs_2_, ...), custom_call_target="tpu_custom_call" | custom-call | flops 4294967296 | bytes 4194304 | tf_op jit(solution)/shard_map/pallas_call | solution.py:515
  65.1 0.0 collective-permute-done.11.refs_14_
  65.1 1.9 %collective-permute-start.15 = (bf16[1024,4,128]{2,1,0:T(4,128)(2,1)S(1)}, bf16[1024,4,128]{2,1,0:T(4,128)(2,1)S(1)}, u32[]{:S(2)}, u32[]{:S(2)}) collective-permute-start(bf16[1024,4,128]{2,1,0:T(4,128)(2,1)S(1)} %collective-permute-done.11.refs_14_), channel_id=1, source_target_pairs={{32,0},{33,1},{34,2},{35,3},{36,4},{37,5},{38,6},{39,7},{40,8},{41... | collective-permute-start | bytes 3145736 | tf_op jit(solution)/shard_map/ppermute | solution.py:63
  67.0 3.6 %shard_map.216 = (bf16[4096,512]{1,0:T(8,128)(2,1)S(1)}, f32[512,512]{1,0:T(8,128)S(1)}) custom-call(s32[4,1,1024]{2,1,0:T(1,128)S(1)} %get-tuple-element.58.snd_ref.refs_0_, s32[4,1,1024]{2,1,0:T(1,128)S(1)} %get-tuple-element.59.rcv_ref.refs_1_, ...), custom_call_target="tpu_custom_call", output_to_operand_aliasing={{0}: (11, {}), {1}: (12, {})} | custom-call | flops 2147483648 | bytes 2097152 | tf_op jit(solution)/shard_map/pallas_call | solution.py:515
  70.6 0.0 collective-permute-done.13.refs_16_
  70.6 0.0 collective-permute-done.12.refs_15_
  70.6 0.1 collective-permute-start.16
  70.7 0.5 collective-permute-start.17
  71.2 0.0 collective-permute-done.14.refs_17_
  71.2 0.0 collective-permute-done.15.refs_18_
  71.2 0.0 copy-start.1
  71.2 4.3 %shard_map.217 = (bf16[4096,512]{1,0:T(8,128)(2,1)S(1)}, f32[512,512]{1,0:T(8,128)S(1)}, bf16[8192,4,128]{2,1,0:T(4,128)(2,1)S(1)}) custom-call(s32[4,1,1024]{2,1,0:T(1,128)S(1)} %get-tuple-element.58.snd_ref.refs_0_, s32[4,1,1024]{2,1,0:T(1,128)S(1)} %get-tuple-element.59.rcv_ref.refs_1_, ...), custom_call_target="tpu_custom_call", output_to_operand_aliasing={{0}: (11, {}), {1}: (12, {})} | custom-call | flops 2147483648 | bytes 2097152 | tf_op jit(solution)/shard_map/pallas_call | solution.py:515
  75.5 0.0 collective-permute-done.16.refs_1_
  75.5 0.0 collective-permute-done.17.refs_2_
  75.5 0.0 copy-done.1
  75.5 12.7 %shard_map.218 = (f32[512,512]{1,0:T(8,128)}, bf16[4096,512]{1,0:T(8,128)(2,1)}, bf16[8192,4,128]{2,1,0:T(4,128)(2,1)S(1)}, bf16[4096,512]{1,0:T(8,128)(2,1)S(1)}) custom-call(s32[16]{0:T(128)S(1)} %get-tuple-element.72.info_ref, s32[18,1,256]{2,1,0:T(1,128)S(1)} %get-tuple-element.73.code_ref, ...), custom_call_target="tpu_custom_call", output_to_operand_aliasing={{2}: (2, {}), {3}: (5, {})} | custom-call | flops 4294967296 | bytes 25165824 | tf_op jit(solution)/shard_map/pallas_call | solution.py:528
  (2 shorter events, 0.1 us)
Async XLA Ops:
  1.5 13.8 %collective-permute-start = (bf16[32,4,128]{2,1,0:T(4,128)(2,1)S(1)}, bf16[32,4,128]{2,1,0:T(4,128)(2,1)S(1)}, u32[]{:S(2)}, u32[]{:S(2)}) collective-permute-start(bf16[32,4,128]{2,1,0:T(4,128)(2,1)S(1)} %reshape.39), channel_id=1, source_target_pairs={{4,0},{5,1},{6,2},{7,3},{0,4},{1,5},{2,6},{3,7},{12,8},{13,9},{14,... | collective-permute-start | bytes 98312 | tf_op jit(solution)/shard_map/ppermute | solution.py:63
  9.4 1.2 %copy-start = (f32[512,512]{1,0:T(8,128)S(1)}, f32[512,512]{1,0:T(8,128)}, u32[]{:S(2)}) copy-start(f32[512,512]{1,0:T(8,128)} %refs_9_.3) | copy-start | bytes 3145732
  10.6 0.7 copy-start.2
  12.4 4.1 %collective-permute-start.1 = (bf16[64,512]{1,0:T(8,128)(2,1)S(1)}, bf16[64,512]{1,0:T(8,128)(2,1)S(1)}, u32[]{:S(2)}, u32[]{:S(2)}) collective-permute-start(bf16[64,512]{1,0:T(8,128)(2,1)S(1)} %get-tuple-element.54), channel_id=1, source_target_pairs={{224,0},{225,1},{226,2},{227,3},{228,4},{229,5},{230,6},{231,7},{2... | collective-permute-start | bytes 196616 | tf_op jit(solution)/shard_map/ppermute | solution.py:63
  14.5 2.0 %collective-permute-start.2 = (bf16[64,512]{1,0:T(8,128)(2,1)S(1)}, bf16[64,512]{1,0:T(8,128)(2,1)S(1)}, u32[]{:S(2)}, u32[]{:S(2)}) collective-permute-start(bf16[64,512]{1,0:T(8,128)(2,1)S(1)} %get-tuple-element.55), channel_id=1, source_target_pairs={{32,0},{33,1},{34,2},{35,3},{36,4},{37,5},{38,6},{39,7},{40,8},{41... | collective-permute-start | bytes 196616 | tf_op jit(solution)/shard_map/ppermute | solution.py:63
  16.5 14.6 %collective-permute-start.5 = (bf16[64,4,128]{2,1,0:T(4,128)(2,1)S(1)}, bf16[64,4,128]{2,1,0:T(4,128)(2,1)S(1)}, u32[]{:S(2)}, u32[]{:S(2)}) collective-permute-start(bf16[64,4,128]{2,1,0:T(4,128)(2,1)S(1)} %pad_maximum_fusion.1), channel_id=1, source_target_pairs={{144,0},{145,1},{146,2},{147,3},{148,4},{149,5},{150,6},{151,7},{1... | collective-permute-start | bytes 196616 | tf_op jit(solution)/shard_map/ppermute | solution.py:63
  21.8 9.2 %collective-permute-start.4 = (bf16[64,4,128]{2,1,0:T(4,128)(2,1)S(1)}, bf16[64,4,128]{2,1,0:T(4,128)(2,1)S(1)}, u32[]{:S(2)}, u32[]{:S(2)}) collective-permute-start(bf16[64,4,128]{2,1,0:T(4,128)(2,1)S(1)} %pad_maximum_fusion.1), channel_id=1, source_target_pairs={{16,0},{17,1},{18,2},{19,3},{20,4},{21,5},{22,6},{23,7},{24,8},{25... | collective-permute-start | bytes 196616 | tf_op jit(solution)/shard_map/ppermute | solution.py:63
  22.1 9.0 %collective-permute-start.3 = (bf16[64,4,128]{2,1,0:T(4,128)(2,1)S(1)}, bf16[64,4,128]{2,1,0:T(4,128)(2,1)S(1)}, u32[]{:S(2)}, u32[]{:S(2)}) collective-permute-start(bf16[64,4,128]{2,1,0:T(4,128)(2,1)S(1)} %pad_maximum_fusion.1), channel_id=1, source_target_pairs={{128,0},{129,1},{130,2},{131,3},{132,4},{133,5},{134,6},{135,7},{1... | collective-permute-start | bytes 196616 | tf_op jit(solution)/shard_map/ppermute | solution.py:63
  22.8 8.5 %collective-permute-start.6 = (bf16[64,512]{1,0:T(8,128)(2,1)S(1)}, bf16[64,512]{1,0:T(8,128)(2,1)S(1)}, u32[]{:S(2)}, u32[]{:S(2)}) collective-permute-start(bf16[64,512]{1,0:T(8,128)(2,1)S(1)} %get-tuple-element.63), channel_id=1, source_target_pairs={{31,0},{0,1},{1,2},{2,3},{3,4},{4,5},{5,6},{6,7},{7,8},{8,9},{9,10... | collective-permute-start | bytes 196616 | tf_op jit(solution)/shard_map/ppermute | solution.py:63
  23.6 7.7 %collective-permute-start.7 = (bf16[64,512]{1,0:T(8,128)(2,1)S(1)}, bf16[64,512]{1,0:T(8,128)(2,1)S(1)}, u32[]{:S(2)}, u32[]{:S(2)}) collective-permute-start(bf16[64,512]{1,0:T(8,128)(2,1)S(1)} %get-tuple-element.65), channel_id=1, source_target_pairs={{1,0},{2,1},{3,2},{4,3},{5,4},{6,5},{7,6},{8,7},{9,8},{10,9},{11,1... | collective-permute-start | bytes 196616 | tf_op jit(solution)/shard_map/ppermute | solution.py:63
  31.3 18.7 %collective-permute-start.10 = (bf16[256,4,128]{2,1,0:T(4,128)(2,1)S(1)}, bf16[256,4,128]{2,1,0:T(4,128)(2,1)S(1)}, u32[]{:S(2)}, u32[]{:S(2)}) collective-permute-start(bf16[256,4,128]{2,1,0:T(4,128)(2,1)S(1)} %pad_maximum_fusion), channel_id=1, source_target_pairs={{2,0},{3,1},{4,2},{5,3},{6,4},{7,5},{0,6},{1,7},{10,8},{11,9},{12,... | collective-permute-start | bytes 786440 | tf_op jit(solution)/shard_map/ppermute | solution.py:63
  31.4 18.5 %collective-permute-start.9 = (bf16[256,4,128]{2,1,0:T(4,128)(2,1)S(1)}, bf16[256,4,128]{2,1,0:T(4,128)(2,1)S(1)}, u32[]{:S(2)}, u32[]{:S(2)}) collective-permute-start(bf16[256,4,128]{2,1,0:T(4,128)(2,1)S(1)} %pad_maximum_fusion), channel_id=1, source_target_pairs={{223,0},{216,1},{217,2},{218,3},{219,4},{220,5},{221,6},{222,7},{1... | collective-permute-start | bytes 786440 | tf_op jit(solution)/shard_map/ppermute | solution.py:63
  37.1 12.6 %collective-permute-start.8 = (bf16[256,4,128]{2,1,0:T(4,128)(2,1)S(1)}, bf16[256,4,128]{2,1,0:T(4,128)(2,1)S(1)}, u32[]{:S(2)}, u32[]{:S(2)}) collective-permute-start(bf16[256,4,128]{2,1,0:T(4,128)(2,1)S(1)} %pad_maximum_fusion), channel_id=1, source_target_pairs={{73,0},{74,1},{75,2},{76,3},{77,4},{78,5},{79,6},{72,7},{81,8},{82... | collective-permute-start | bytes 786440 | tf_op jit(solution)/shard_map/ppermute | solution.py:63
  50.1 14.9 %collective-permute-start.11 = (bf16[1024,4,128]{2,1,0:T(4,128)(2,1)S(1)}, bf16[1024,4,128]{2,1,0:T(4,128)(2,1)S(1)}, u32[]{:S(2)}, u32[]{:S(2)}) collective-permute-start(bf16[1024,4,128]{2,1,0:T(4,128)(2,1)S(1)} %constant_dynamic-update-slice_fusion.refs_13_), channel_id=1, source_target_pairs={{64,0},{65,1},{66,2},{67,3},{68,4},{69,5},{70,6},{71,7},{72,8},{73... | collective-permute-start | bytes 3145736 | tf_op jit(solution)/shard_map/ppermute | solution.py:63
  50.2 20.3 %collective-permute-start.13 = (bf16[1024,4,128]{2,1,0:T(4,128)(2,1)S(1)}, bf16[1024,4,128]{2,1,0:T(4,128)(2,1)S(1)}, u32[]{:S(2)}, u32[]{:S(2)}) collective-permute-start(bf16[1024,4,128]{2,1,0:T(4,128)(2,1)S(1)} %constant_dynamic-update-slice_fusion.refs_13_), channel_id=1, source_target_pairs={{1,0},{2,1},{3,2},{4,3},{5,4},{6,5},{7,6},{0,7},{9,8},{10,9},{11,1... | collective-permute-start | bytes 3145736 | tf_op jit(solution)/shard_map/ppermute | solution.py:63
  50.3 20.3 %collective-permute-start.12 = (bf16[1024,4,128]{2,1,0:T(4,128)(2,1)S(1)}, bf16[1024,4,128]{2,1,0:T(4,128)(2,1)S(1)}, u32[]{:S(2)}, u32[]{:S(2)}) collective-permute-start(bf16[1024,4,128]{2,1,0:T(4,128)(2,1)S(1)} %constant_dynamic-update-slice_fusion.refs_13_), channel_id=1, source_target_pairs={{8,0},{9,1},{10,2},{11,3},{12,4},{13,5},{14,6},{15,7},{16,8},{17,9... | collective-permute-start | bytes 3145736 | tf_op jit(solution)/shard_map/ppermute | solution.py:63
  50.6 20.6 %collective-permute-start.14 = (bf16[1024,4,128]{2,1,0:T(4,128)(2,1)S(1)}, bf16[1024,4,128]{2,1,0:T(4,128)(2,1)S(1)}, u32[]{:S(2)}, u32[]{:S(2)}) collective-permute-start(bf16[1024,4,128]{2,1,0:T(4,128)(2,1)S(1)} %constant_dynamic-update-slice_fusion.refs_13_), channel_id=1, source_target_pairs={{32,0},{33,1},{34,2},{35,3},{36,4},{37,5},{38,6},{39,7},{40,8},{41... | collective-permute-start | bytes 3145736 | tf_op jit(solution)/shard_map/ppermute | solution.py:63
  65.1 6.1 %collective-permute-start.15 = (bf16[1024,4,128]{2,1,0:T(4,128)(2,1)S(1)}, bf16[1024,4,128]{2,1,0:T(4,128)(2,1)S(1)}, u32[]{:S(2)}, u32[]{:S(2)}) collective-permute-start(bf16[1024,4,128]{2,1,0:T(4,128)(2,1)S(1)} %collective-permute-done.11.refs_14_), channel_id=1, source_target_pairs={{32,0},{33,1},{34,2},{35,3},{36,4},{37,5},{38,6},{39,7},{40,8},{41... | collective-permute-start | bytes 3145736 | tf_op jit(solution)/shard_map/ppermute | solution.py:63
  70.6 4.9 %collective-permute-start.16 = (bf16[1024,4,128]{2,1,0:T(4,128)(2,1)S(1)}, bf16[1024,4,128]{2,1,0:T(4,128)(2,1)S(1)}, u32[]{:S(2)}, u32[]{:S(2)}) collective-permute-start(bf16[1024,4,128]{2,1,0:T(4,128)(2,1)S(1)} %collective-permute-done.12.refs_15_), channel_id=1, source_target_pairs={{32,0},{33,1},{34,2},{35,3},{36,4},{37,5},{38,6},{39,7},{40,8},{41... | collective-permute-start | bytes 3145736 | tf_op jit(solution)/shard_map/ppermute | solution.py:63
  70.7 4.8 %collective-permute-start.17 = (bf16[1024,4,128]{2,1,0:T(4,128)(2,1)S(1)}, bf16[1024,4,128]{2,1,0:T(4,128)(2,1)S(1)}, u32[]{:S(2)}, u32[]{:S(2)}) collective-permute-start(bf16[1024,4,128]{2,1,0:T(4,128)(2,1)S(1)} %collective-permute-done.13.refs_16_), channel_id=1, source_target_pairs={{32,0},{33,1},{34,2},{35,3},{36,4},{37,5},{38,6},{39,7},{40,8},{41... | collective-permute-start | bytes 3145736 | tf_op jit(solution)/shard_map/ppermute | solution.py:63
  71.2 4.3 %copy-start.1 = (f32[512,512]{1,0:T(8,128)S(1)}, f32[512,512]{1,0:T(8,128)}, u32[]{:S(2)}) copy-start(f32[512,512]{1,0:T(8,128)} %refs_9_.3) | copy-start | bytes 3145732
where the time goes:
time: 88.6 us; the launch traced here: 88.4 us
  Pallas kernels  42.7 us (48%)
  starting transfers between devices  36.2 us (41%)
  waiting for transfers between devices  4.18 us (5%)
  local copies, waits for them, and re-layouts  3.22 us (4%)
  between operations  1.04 us (1%)
  other arithmetic  1.01 us (1%)
    ppermute x18, starting transfers between devices, receive(): lax.ppermute(block, AXES, [(device(*source(*spot)), device(*spot)) for sp...  36.2 us
    pallas_call x3, Pallas kernels, near(): pl.pallas_call(functools.partial(near_kernel, begin, end, pieces), in_spe...  16.1 us
    pallas_call x1, Pallas kernels, far(): pl.pallas_call(far_kernel, in_specs=[SMEM] * 2 + [VMEM] + [ANY] * LATE +...  12.7 us
    pallas_call x1, Pallas kernels, compact(): pl.pallas_call(compact_kernel, in_specs=[SMEM] + [VMEM] * (len(args) - 1)...  9.44 us
    ppermute x18, waiting for transfers between devices, receive(): lax.ppermute(block, AXES, [(device(*source(*spot)), device(*spot)) for sp...  4.18 us
    pallas_call x1, Pallas kernels, load(): pl.pallas_call(load_kernel, in_specs=[HBM] * count, out_specs=[VMEM] * co...  3.42 us
    unnamed x9, local copies, waits for them, and re-layouts  2.23 us
  transfers between devices with their start and end apart: 18, of which 2 were waited for; matrix products, arithmetic and copies ran while one was open for 2% of the time, Pallas kernels for 34%

commit v1 on v0

--- a/solution.py
+++ b/solution.py
@@ -110,7 +110,16 @@
     return lax.broadcasted_iota(jnp.int32, shape, dim)
 
 
-def pick_kernel(spot_ref, nodes_ref, rows_ref, own_ref, *out_refs):
+def pick_kernel(spot_ref, nodes_in, rows_in, nodes_ref, own_ref, *refs):
+    out_refs = refs[:4]
+    rows_ref, sems = refs[4:]
+    copies = [
+        pltpu.make_async_copy(nodes_in, nodes_ref, sems.at[0]), pltpu.make_async_copy(rows_in, rows_ref, sems.at[1]),
+    ]
+    for copy in copies:
+        copy.start()
+    for copy in copies:
+        copy.wait()
     own = nodes_ref[...].astype(BF16)
     own_ref[...] = own
     core = spot_ref[3]
@@ -126,7 +135,7 @@
 ):
     ts_ref[...] = dot(own_ref[...], w_sender_ref[...]).astype(BF16)
     tr_ref[...] = dot(own_ref[...], w_receiver_ref[...]).astype(BF16)
-    upper[...] = (iota((TILE, TILE), 0) < iota((TILE, TILE), 1)).astype(BF16)
+    upper[...] = (iota((256, 256), 0) < iota((256, 256), 1)).astype(BF16)
     rcv_out_ref[...] = jnp.full_like(rcv_out_ref, NODE)
     count[0] = 0
 
@@ -185,7 +194,12 @@
     place = (((p >> 5) & 1) << 7) | (dx << 5) | (dy << 3) | dz
     far_f = far.astype(F32)
     base = count[0]
-    before = dot(jnp.broadcast_to(far_f, (8, TILE)).astype(BF16), upper[...])[0:1].astype(jnp.int32)
+    wide = jnp.broadcast_to(far_f, (8, TILE)).astype(BF16)
+    before, passed = [], jnp.zeros((1, 1), F32)
+    for k in range(0, TILE, 256):
+        before.append(dot(wide[:, k:k + 256], upper[...])[0:1] + passed)
+        passed = passed + jnp.sum(far_f[:, k:k + 256], axis=1, keepdims=True)
+    before = jnp.concatenate(before, axis=1).astype(jnp.int32)
     number = jnp.sum(far_f).astype(jnp.int32)
     slot = jnp.where(far, base + before, -1)
     slot_ref[t] = slot
@@ -357,10 +371,9 @@
         row = b * (SLOTS // BLOCK)
 
         def gather(i, c):
+            at, col, there = row + (i >> 4), (i & 15) * 16, pl.multiple_of(i * 64, 64)
             for k in range(16):
-                slot = i * 16 + k
-                code = code_ref[row + (slot >> 8), 0, slot & 255]
-                rows_buf[pl.ds(pl.multiple_of(slot * 4, 4), 4)] = table[code].astype(F32)
+                rows_buf[pl.ds(there + k * 4, 4)] = table[code_ref[at, 0, col + k]].astype(F32)
             return c
 
         lax.fori_loop(0, count // 16, gather, 0)
@@ -383,7 +396,9 @@
             agg[...] += dot(hot, update.astype(BF16))
         return carry
 
-    lax.fori_loop(0, (total + SLOTS - 1) // SLOTS, block, 0)
+    blocks = (total + SLOTS - 1) // SLOTS
+    lax.fori_loop(0, blocks, block, 0)
+    new_far[pl.ds(pl.multiple_of(blocks * SLOTS, SLOTS), BLOCK)] = jnp.zeros((BLOCK, D), BF16)
 
     def store(t):
         rows = pl.ds(pl.multiple_of(t * TILE, TILE), TILE)
@@ -398,13 +413,26 @@
         slots = jnp.concatenate([slot_ref[t]] * 8, axis=0).astype(F32)
         slots = jnp.transpose(slots, (1, 0)).astype(jnp.int32)[:, 0:1]
 
-        def scatter(b, c):
-            hot = (iota((TILE, BLOCK), 1) + b * BLOCK == slots).astype(BF16)
-            there = pl.ds(pl.multiple_of(b * BLOCK, BLOCK), BLOCK)
+        start = base // 16 * 16
+        fits = end - start <= BLOCK
+
+        def scatter(start):
+            hot = (iota((TILE, BLOCK), 1) + start == slots).astype(BF16)
+            there = pl.ds(pl.multiple_of(start, 16), BLOCK)
             near[rows] = near[rows] + dot(hot, new_far[there]).astype(BF16)
-            return c
-
-        lax.fori_loop(first, last, scatter, 0)
+
+        @pl.when(jnp.logical_and(end > base, fits))
+        def _():
+            scatter(start)
+
+        @pl.when(jnp.logical_not(fits))
+        def _():
+            def some(b, c):
+                scatter(b * BLOCK)
+                return c
+
+            lax.fori_loop(first, last, some, 0)
+
         store(t).start()
         return carry
 
@@ -471,12 +499,13 @@
 def pick(spot, nodes, send_rows):
     return pl.pallas_call(
         pick_kernel,
-        in_specs=[SMEM, VMEM, VMEM],
-        out_specs=[VMEM] * 5,
-        out_shape=(kept((NODE, D), BF16),) + (shape((HALO, D), BF16),) * 4,
+        in_specs=[SMEM, HBM, HBM],
+        out_specs=[VMEM] * 6,
+        out_shape=(kept((NODE, D), F32), kept((NODE, D), BF16)) + (shape((HALO, D), BF16),) * 4,
+        scratch_shapes=[pltpu.VMEM((4, HALO), jnp.int32), pltpu.SemaphoreType.DMA((2,))],
         compiler_params=pltpu.CompilerParams(vmem_limit_bytes=16 << 20),
         cost_estimate=pl.CostEstimate(flops=2 * NODE * D * 256, bytes_accessed=2 << 20, transcendentals=0),
-    )(spot, nodes, send_rows)
+    )(spot, far_away(nodes), far_away(send_rows))
 
 
 def compact(*args):
@@ -492,7 +521,7 @@
             pltpu.HBM((rows, D), BF16), pltpu.HBM((rows, D), F32),
         ),
         scratch_shapes=[
-            pltpu.VMEM((TILE, TILE), BF16), pltpu.VMEM((rows, D), BF16),
+            pltpu.VMEM((256, 256), BF16), pltpu.VMEM((rows, D), BF16),
             pltpu.VMEM((BLOCKS, 8, BLOCK), F32), pltpu.VMEM((rows, D), F32),
             pltpu.SMEM((1,), jnp.int32), pltpu.SemaphoreType.DMA((BLOCKS, 2)),
         ],
@@ -533,7 +562,7 @@
         input_output_aliases={2: 2, 3 + LATE: 3},
         scratch_shapes=[
             pltpu.VMEM((4 * SLOTS, 128), F32),
-            pltpu.VMEM((SLOTS, D), BF16), pltpu.VMEM((SLOTS, D), F32), pltpu.VMEM((BLOCKS * BLOCK, D), BF16),
+            pltpu.VMEM((SLOTS, D), BF16), pltpu.VMEM((SLOTS, D), F32), pltpu.VMEM(((BLOCKS + 1) * BLOCK, D), BF16),
             pltpu.VMEM((NODE, D), F32),
             pltpu.SemaphoreType.DMA((LATE,)), pltpu.SemaphoreType.DMA((TILES,)), pltpu.SemaphoreType.DMA((2,)),
         ],
@@ -553,9 +582,8 @@
     x, c, y, z = (lax.axis_index(a) for a in AXES)
     spot = jnp.stack([x, y, z, c]).astype(jnp.int32)
     held = nodes[:COARSE_DEV].astype(BF16).reshape(COARSE_DEV, 4, 128)
-    nodes = keep(nodes)
-    own, *out = pick(spot, nodes, send_rows)
-    own = keep(own)
+    nodes, own, *out = pick(spot, nodes, send_rows)
+    nodes, own = keep(nodes), keep(own)
     tables = jnp.asarray(np.repeat(PLACES.reshape(2, 1, 256), 8, axis=1), BF16)
     place = jnp.where(c == 0, tables[0], tables[1])
 
@@ -563,9 +591,8 @@
         got = [from_chip(held, pair) for pair in stage]
         return jnp.concatenate([after(held, *first)] + got, axis=0)
 
-    across = [next_chip(out[2]), other_core(out[3])]
-    held = after(grow(held, STAGES[0]), *across)
-    halo = [shift_patch(after(out[0], held), 1), shift_patch(after(out[1], held), -1)] + across
+    held = after(grow(held, STAGES[0]), own)
+    halo = [shift_patch(after(out[0], held), 1), shift_patch(after(out[1], held), -1)]
     names = load(
         after(edges, held), tiles(sender), tiles(receiver), w_sender, w_edge, w_edge2, w_receiver,
         w_node_self, w_node_aggr, w_node2,
@@ -583,11 +610,12 @@
         return [keep(v) for v in outs]
 
     held = after(grow(held, STAGES[1]), edges, *halo)
+    halo = halo + [next_chip(after(out[2], held)), other_core(after(out[3], held))]
     slot, info, far_code, far_rcv, own_ts, tr, far_edges, far_pre = compact(
         spot, snd, rcv, edges, keep(after(own, held)), w_sender, w_receiver, w_edge, bias_edge1, place,
     )
     slot, far_rcv, own_ts, tr = (keep(v) for v in (slot, far_rcv, own_ts, tr))
-    held = grow(held, STAGES[2], tr)
+    held = grow(held, STAGES[2], tr, *halo)
     last = [from_chip(held, pair) for pair in LAST]
     done, agg, ts = edge_part(0, 2, 0, spot, keep(after(own_ts, held)), *halo, w_sender)
     first = [other_core(held), other_core(after(last[0], agg))]

time: 88.6 us -> 82.8 us (0.935)
  waiting for transfers between devices: 4.18 us -> 1.3 us
  local copies, waits for them, and re-layouts: 3.22 us -> 1.31 us
  Pallas kernels: 42.7 us -> 41.4 us
    ppermute x18, waiting for transfers between devices: 4.18 us -> 1.3 us  [receive(): lax.ppermute(block, AXES, [(device(*source(*spot)), device(*spot)) for sp...]
    unnamed x9 -> x3, local copies, waits for them, and re-layouts: 2.23 us -> 0.33 us
    pallas_call x1, Pallas kernels: 12.7 us -> 11.2 us  [far(): pl.pallas_call(far_kernel, in_specs=[SMEM] * 2 + [VMEM] + [ANY] * LATE +...]
    pallas_call x1, Pallas kernels: 1.05 us -> 2.3 us  [pick(): pl.pallas_call(pick_kernel, in_specs=[SMEM, HBM, HBM], out_specs=[VMEM] *...]
    pallas_call x1, Pallas kernels: 9.44 us -> 8.37 us  [compact(): pl.pallas_call(compact_kernel, in_specs=[SMEM] + [VMEM] * (len(args) - 1)...]
  transfers between devices with their start and end apart: 18 -> 18, of which waited for: 2 -> 1; matrix products, arithmetic and copies ran while one was open for 2% -> 2% of each run, Pallas kernels for 34% -> 37%
where the time goes in v1:
time: 82.8 us; the launch traced here: 82.5 us
  Pallas kernels  41.4 us (50%)
  starting transfers between devices  36.4 us (44%)
  local copies, waits for them, and re-layouts  1.31 us (2%)
  waiting for transfers between devices  1.3 us (2%)
  between operations  1.03 us (1%)
  other arithmetic  1.02 us (1%)
    ppermute x18, starting transfers between devices, receive(): lax.ppermute(block, AXES, [(device(*source(*spot)), device(*spot)) for sp...  36.4 us
    pallas_call x3, Pallas kernels, near(): pl.pallas_call(functools.partial(near_kernel, begin, end, pieces), in_spe...  16.1 us
    pallas_call x1, Pallas kernels, far(): pl.pallas_call(far_kernel, in_specs=[SMEM] * 2 + [VMEM] + [ANY] * LATE +...  11.2 us
    pallas_call x1, Pallas kernels, compact(): pl.pallas_call(compact_kernel, in_specs=[SMEM] + [VMEM] * (len(args) - 1)...  8.37 us
    pallas_call x1, Pallas kernels, load(): pl.pallas_call(load_kernel, in_specs=[HBM] * count, out_specs=[VMEM] * co...  3.42 us
    pallas_call x1, Pallas kernels, pick(): pl.pallas_call(pick_kernel, in_specs=[SMEM, HBM, HBM], out_specs=[VMEM] *...  2.3 us
  transfers between devices with their start and end apart: 18, of which 1 were waited for; matrix products, arithmetic and copies ran while one was open for 2% of the time, Pallas kernels for 37%

profile of v1, /device:TPU:1, one launch (start us, length us, event | category | flops | bytes accessed | tf_op | source)
XLA Modules:
  0.0 82.5 jit_solution(13062983680476247780)
XLA Ops:
  0.6 0.8 %slice.15 = bf16[32,512]{1,0:T(8,128)(2,1)S(1)} slice(f32[512,512]{1,0:T(8,128)} %nodes_in.1), slice={[0:32], [0:512]} | slice | bytes 65536 | tf_op jit(solution)/shard_map/slice | solution.py:584
  1.5 7.8 %collective-permute-start = (bf16[32,4,128]{2,1,0:T(4,128)(2,1)S(1)}, bf16[32,4,128]{2,1,0:T(4,128)(2,1)S(1)}, u32[]{:S(2)}, u32[]{:S(2)}) collective-permute-start(bf16[32,4,128]{2,1,0:T(4,128)(2,1)S(1)} %reshape.39), channel_id=1, source_target_pairs={{4,0},{5,1},{6,2},{7,3},{0,4},{1,5},{2,6},{3,7},{12,8},{13,9},{14,... | collective-permute-start | bytes 98312 | tf_op jit(solution)/shard_map/ppermute | solution.py:63
  9.3 0.1 pad_add_fusion.spot_ref.refs_10_
  9.4 2.3 %shard_map.212 = (f32[512,512]{1,0:T(8,128)S(1)}, bf16[512,512]{1,0:T(8,128)(2,1)S(1)}, bf16[64,512]{1,0:T(8,128)(2,1)S(1)}, bf16[64,512]{1,0:T(8,128)(2,1)S(1)}...) custom-call(s32[4]{0:T(128)S(1)} %pad_add_fusion.spot_ref.refs_10_, f32[512,512]{1,0:T(8,128)} %nodes_in.1, ...), custom_call_target="tpu_custom_call" | custom-call | flops 134217728 | bytes 2097152 | tf_op jit(solution)/shard_map/pallas_call | solution.py:500
  11.7 0.0 collective-permute-done
  11.8 5.5 %collective-permute-start.3 = (bf16[64,4,128]{2,1,0:T(4,128)(2,1)S(1)}, bf16[64,4,128]{2,1,0:T(4,128)(2,1)S(1)}, u32[]{:S(2)}, u32[]{:S(2)}) collective-permute-start(bf16[64,4,128]{2,1,0:T(4,128)(2,1)S(1)} %pad_maximum_fusion.1), channel_id=1, source_target_pairs={{144,0},{145,1},{146,2},{147,3},{148,4},{149,5},{150,6},{151,7},{1... | collective-permute-start | bytes 196616 | tf_op jit(solution)/shard_map/ppermute | solution.py:63
  17.2 0.2 collective-permute-start.2
  17.5 0.2 collective-permute-start.1
  17.6 0.7 select_bitcast_fusion.place_ref
  18.3 0.7 collective-permute-start.4
  19.0 4.6 %collective-permute-start.5 = (bf16[64,512]{1,0:T(8,128)(2,1)S(1)}, bf16[64,512]{1,0:T(8,128)(2,1)S(1)}, u32[]{:S(2)}, u32[]{:S(2)}) collective-permute-start(bf16[64,512]{1,0:T(8,128)(2,1)S(1)} %get-tuple-element.66), channel_id=1, source_target_pairs={{1,0},{2,1},{3,2},{4,3},{5,4},{6,5},{7,6},{8,7},{9,8},{10,9},{11,1... | collective-permute-start | bytes 196616 | tf_op jit(solution)/shard_map/ppermute | solution.py:63
  23.6 3.4 %shard_map.213 = (bf16[4096,512]{1,0:T(8,128)(2,1)S(1)}, s32[4,1,1024]{2,1,0:T(1,128)S(1)}, s32[4,1,1024]{2,1,0:T(1,128)S(1)}, bf16[512,512]{1,0:T(8,128)(2,1)S(...) custom-call(bf16[4096,512]{1,0:T(8,128)(2,1)} %refs_0_, ...), custom_call_target="tpu_custom_call" | custom-call | bytes 16777216 | tf_op jit(solution)/shard_map/pallas_call | solution.py:488
  27.1 0.0 collective-permute-done.3
  27.1 0.0 collective-permute-done.2
  27.1 0.0 collective-permute-done.1
  27.1 0.2 pad_maximum_fusion
  27.3 0.0 collective-permute-done.4.refs_12_
  27.3 0.0 collective-permute-done.5.refs_13_
  27.3 0.1 collective-permute-start.10
  27.4 4.9 %collective-permute-start.9 = (bf16[256,4,128]{2,1,0:T(4,128)(2,1)S(1)}, bf16[256,4,128]{2,1,0:T(4,128)(2,1)S(1)}, u32[]{:S(2)}, u32[]{:S(2)}) collective-permute-start(bf16[256,4,128]{2,1,0:T(4,128)(2,1)S(1)} %pad_maximum_fusion), channel_id=1, source_target_pairs={{223,0},{216,1},{217,2},{218,3},{219,4},{220,5},{221,6},{222,7},{1... | collective-permute-start | bytes 786440 | tf_op jit(solution)/shard_map/ppermute | solution.py:63
  32.3 0.0 collective-permute-start.8
  32.3 5.5 %collective-permute-start.6 = (bf16[64,512]{1,0:T(8,128)(2,1)S(1)}, bf16[64,512]{1,0:T(8,128)(2,1)S(1)}, u32[]{:S(2)}, u32[]{:S(2)}) collective-permute-start(bf16[64,512]{1,0:T(8,128)(2,1)S(1)} %get-tuple-element.82), channel_id=1, source_target_pairs={{224,0},{225,1},{226,2},{227,3},{228,4},{229,5},{230,6},{231,7},{2... | collective-permute-start | bytes 196616 | tf_op jit(solution)/shard_map/ppermute | solution.py:63
  37.8 0.1 collective-permute-start.7
  37.9 8.4 %shard_map.214 = (s32[4,1,1024]{2,1,0:T(1,128)S(1)}, s32[16]{0:T(128)S(1)}, s32[18,1,256]{2,1,0:T(1,128)S(1)}, s32[18,1,256]{2,1,0:T(1,128)S(1)}, bf16[512,512]{...) custom-call(s32[4]{0:T(128)S(1)} %pad_add_fusion.spot_ref.refs_10_, ...), custom_call_target="tpu_custom_call" | custom-call | flops 4294967296 | bytes 8388608 | tf_op jit(solution)/shard_map/pallas_call | solution.py:513
  46.3 0.0 collective-permute-done.6.refs_14_
  46.3 0.0 collective-permute-done.7.refs_15_
  46.3 0.1 constant_dynamic-update-slice_fusion.3
  46.4 0.0 collective-permute-done.8
  46.4 0.1 constant_dynamic-update-slice_fusion.2
  46.5 0.0 collective-permute-done.9
  46.5 0.1 constant_dynamic-update-slice_fusion.1
  46.7 0.0 collective-permute-done.10
  46.7 0.1 constant_dynamic-update-slice_fusion.refs_13_
  46.8 1.2 %collective-permute-start.11 = (bf16[1024,4,128]{2,1,0:T(4,128)(2,1)S(1)}, bf16[1024,4,128]{2,1,0:T(4,128)(2,1)S(1)}, u32[]{:S(2)}, u32[]{:S(2)}) collective-permute-start(bf16[1024,4,128]{2,1,0:T(4,128)(2,1)S(1)} %constant_dynamic-update-slice_fusion.refs_13_), channel_id=1, source_target_pairs={{64,0},{65,1},{66,2},{67,3},{68,4},{69,5},{70,6},{71,7},{72,8},{73... | collective-permute-start | bytes 3145736 | tf_op jit(solution)/shard_map/ppermute | solution.py:63
  48.0 0.2 collective-permute-start.13
  48.1 0.1 collective-permute-start.12
  48.2 4.0 %collective-permute-start.14 = (bf16[1024,4,128]{2,1,0:T(4,128)(2,1)S(1)}, bf16[1024,4,128]{2,1,0:T(4,128)(2,1)S(1)}, u32[]{:S(2)}, u32[]{:S(2)}) collective-permute-start(bf16[1024,4,128]{2,1,0:T(4,128)(2,1)S(1)} %constant_dynamic-update-slice_fusion.refs_13_), channel_id=1, source_target_pairs={{32,0},{33,1},{34,2},{35,3},{36,4},{37,5},{38,6},{39,7},{40,8},{41... | collective-permute-start | bytes 3145736 | tf_op jit(solution)/shard_map/ppermute | solution.py:63
  52.3 8.2 %shard_map.215 = (bf16[4096,512]{1,0:T(8,128)(2,1)S(1)}, f32[512,512]{1,0:T(8,128)S(1)}, bf16[768,512]{1,0:T(8,128)(2,1)S(1)}) custom-call(s32[4,1,1024]{2,1,0:T(1,128)S(1)} %get-tuple-element.60.snd_ref.refs_0_, s32[4,1,1024]{2,1,0:T(1,128)S(1)} %get-tuple-element.61.rcv_ref.refs_1_, bf16[4096,512]{1,0:T(8,128)(2,1)S(1)} %get-tuple-element.62.edges_ref.refs_2_, ...), custom_call_target="tpu_custom_call" | custom-call | flops 4294967296 | bytes 4194304 | tf_op jit(solution)/shard_map/pallas_call | solution.py:544
  60.5 1.3 %collective-permute-done.11.refs_14_ = bf16[1024,4,128]{2,1,0:T(4,128)(2,1)S(1)} collective-permute-done((bf16[1024,4,128]{2,1,0:T(4,128)(2,1)S(1)}, bf16[1024,4,128]{2,1,0:T(4,128)(2,1)S(1)}, u32[]{:S(2)}, u32[]{:S(2)}) %collective-permute-start.11) | collective-permute-done | bytes 1048608 | tf_op jit(solution)/shard_map/ppermute | solution.py:63
  61.7 0.8 collective-permute-start.15
  62.5 3.6 %shard_map.216 = (bf16[4096,512]{1,0:T(8,128)(2,1)S(1)}, f32[512,512]{1,0:T(8,128)S(1)}) custom-call(s32[4,1,1024]{2,1,0:T(1,128)S(1)} %get-tuple-element.60.snd_ref.refs_0_, s32[4,1,1024]{2,1,0:T(1,128)S(1)} %get-tuple-element.61.rcv_ref.refs_1_, ...), custom_call_target="tpu_custom_call", output_to_operand_aliasing={{0}: (11, {}), {1}: (12, {})} | custom-call | flops 2147483648 | bytes 2097152 | tf_op jit(solution)/shard_map/pallas_call | solution.py:544
  66.1 0.0 collective-permute-done.13.refs_16_
  66.1 0.0 collective-permute-done.12.refs_15_
  66.2 0.1 collective-permute-start.16
  66.3 0.5 collective-permute-start.17
  66.7 0.0 collective-permute-done.14.refs_17_
  66.8 0.0 collective-permute-done.15.refs_18_
  66.8 4.3 %shard_map.217 = (bf16[4096,512]{1,0:T(8,128)(2,1)S(1)}, f32[512,512]{1,0:T(8,128)S(1)}, bf16[8192,4,128]{2,1,0:T(4,128)(2,1)S(1)}) custom-call(s32[4,1,1024]{2,1,0:T(1,128)S(1)} %get-tuple-element.60.snd_ref.refs_0_, s32[4,1,1024]{2,1,0:T(1,128)S(1)} %get-tuple-element.61.rcv_ref.refs_1_, ...), custom_call_target="tpu_custom_call", output_to_operand_aliasing={{0}: (11, {}), {1}: (12, {})} | custom-call | flops 2147483648 | bytes 2097152 | tf_op jit(solution)/shard_map/pallas_call | solution.py:544
  71.1 0.0 collective-permute-done.16.refs_1_
  71.1 0.0 collective-permute-done.17.refs_2_
  71.1 11.2 %shard_map.218 = (f32[512,512]{1,0:T(8,128)}, bf16[4096,512]{1,0:T(8,128)(2,1)}, bf16[8192,4,128]{2,1,0:T(4,128)(2,1)S(1)}, bf16[4096,512]{1,0:T(8,128)(2,1)S(1)}) custom-call(s32[16]{0:T(128)S(1)} %get-tuple-element.73.info_ref, s32[18,1,256]{2,1,0:T(1,128)S(1)} %get-tuple-element.74.code_ref, ...), custom_call_target="tpu_custom_call", output_to_operand_aliasing={{2}: (2, {}), {3}: (5, {})} | custom-call | flops 4294967296 | bytes 25165824 | tf_op jit(solution)/shard_map/pallas_call | solution.py:557
  (2 shorter events, 0.1 us)
Async XLA Ops:
  1.5 10.2 %collective-permute-start = (bf16[32,4,128]{2,1,0:T(4,128)(2,1)S(1)}, bf16[32,4,128]{2,1,0:T(4,128)(2,1)S(1)}, u32[]{:S(2)}, u32[]{:S(2)}) collective-permute-start(bf16[32,4,128]{2,1,0:T(4,128)(2,1)S(1)} %reshape.39), channel_id=1, source_target_pairs={{4,0},{5,1},{6,2},{7,3},{0,4},{1,5},{2,6},{3,7},{12,8},{13,9},{14,... | collective-permute-start | bytes 98312 | tf_op jit(solution)/shard_map/ppermute | solution.py:63
  11.8 15.3 %collective-permute-start.3 = (bf16[64,4,128]{2,1,0:T(4,128)(2,1)S(1)}, bf16[64,4,128]{2,1,0:T(4,128)(2,1)S(1)}, u32[]{:S(2)}, u32[]{:S(2)}) collective-permute-start(bf16[64,4,128]{2,1,0:T(4,128)(2,1)S(1)} %pad_maximum_fusion.1), channel_id=1, source_target_pairs={{144,0},{145,1},{146,2},{147,3},{148,4},{149,5},{150,6},{151,7},{1... | collective-permute-start | bytes 196616 | tf_op jit(solution)/shard_map/ppermute | solution.py:63
  17.2 9.8 %collective-permute-start.2 = (bf16[64,4,128]{2,1,0:T(4,128)(2,1)S(1)}, bf16[64,4,128]{2,1,0:T(4,128)(2,1)S(1)}, u32[]{:S(2)}, u32[]{:S(2)}) collective-permute-start(bf16[64,4,128]{2,1,0:T(4,128)(2,1)S(1)} %pad_maximum_fusion.1), channel_id=1, source_target_pairs={{16,0},{17,1},{18,2},{19,3},{20,4},{21,5},{22,6},{23,7},{24,8},{25... | collective-permute-start | bytes 196616 | tf_op jit(solution)/shard_map/ppermute | solution.py:63
  17.5 9.6 %collective-permute-start.1 = (bf16[64,4,128]{2,1,0:T(4,128)(2,1)S(1)}, bf16[64,4,128]{2,1,0:T(4,128)(2,1)S(1)}, u32[]{:S(2)}, u32[]{:S(2)}) collective-permute-start(bf16[64,4,128]{2,1,0:T(4,128)(2,1)S(1)} %pad_maximum_fusion.1), channel_id=1, source_target_pairs={{128,0},{129,1},{130,2},{131,3},{132,4},{133,5},{134,6},{135,7},{1... | collective-permute-start | bytes 196616 | tf_op jit(solution)/shard_map/ppermute | solution.py:63
  18.3 9.0 %collective-permute-start.4 = (bf16[64,512]{1,0:T(8,128)(2,1)S(1)}, bf16[64,512]{1,0:T(8,128)(2,1)S(1)}, u32[]{:S(2)}, u32[]{:S(2)}) collective-permute-start(bf16[64,512]{1,0:T(8,128)(2,1)S(1)} %get-tuple-element.64), channel_id=1, source_target_pairs={{31,0},{0,1},{1,2},{2,3},{3,4},{4,5},{5,6},{6,7},{7,8},{8,9},{9,10... | collective-permute-start | bytes 196616 | tf_op jit(solution)/shard_map/ppermute | solution.py:63
  19.0 8.3 %collective-permute-start.5 = (bf16[64,512]{1,0:T(8,128)(2,1)S(1)}, bf16[64,512]{1,0:T(8,128)(2,1)S(1)}, u32[]{:S(2)}, u32[]{:S(2)}) collective-permute-start(bf16[64,512]{1,0:T(8,128)(2,1)S(1)} %get-tuple-element.66), channel_id=1, source_target_pairs={{1,0},{2,1},{3,2},{4,3},{5,4},{6,5},{7,6},{8,7},{9,8},{10,9},{11,1... | collective-permute-start | bytes 196616 | tf_op jit(solution)/shard_map/ppermute | solution.py:63
  27.3 19.3 %collective-permute-start.10 = (bf16[256,4,128]{2,1,0:T(4,128)(2,1)S(1)}, bf16[256,4,128]{2,1,0:T(4,128)(2,1)S(1)}, u32[]{:S(2)}, u32[]{:S(2)}) collective-permute-start(bf16[256,4,128]{2,1,0:T(4,128)(2,1)S(1)} %pad_maximum_fusion), channel_id=1, source_target_pairs={{2,0},{3,1},{4,2},{5,3},{6,4},{7,5},{0,6},{1,7},{10,8},{11,9},{12,... | collective-permute-start | bytes 786440 | tf_op jit(solution)/shard_map/ppermute | solution.py:63
  27.4 19.1 %collective-permute-start.9 = (bf16[256,4,128]{2,1,0:T(4,128)(2,1)S(1)}, bf16[256,4,128]{2,1,0:T(4,128)(2,1)S(1)}, u32[]{:S(2)}, u32[]{:S(2)}) collective-permute-start(bf16[256,4,128]{2,1,0:T(4,128)(2,1)S(1)} %pad_maximum_fusion), channel_id=1, source_target_pairs={{223,0},{216,1},{217,2},{218,3},{219,4},{220,5},{221,6},{222,7},{1... | collective-permute-start | bytes 786440 | tf_op jit(solution)/shard_map/ppermute | solution.py:63
  32.3 14.1 %collective-permute-start.8 = (bf16[256,4,128]{2,1,0:T(4,128)(2,1)S(1)}, bf16[256,4,128]{2,1,0:T(4,128)(2,1)S(1)}, u32[]{:S(2)}, u32[]{:S(2)}) collective-permute-start(bf16[256,4,128]{2,1,0:T(4,128)(2,1)S(1)} %pad_maximum_fusion), channel_id=1, source_target_pairs={{73,0},{74,1},{75,2},{76,3},{77,4},{78,5},{79,6},{72,7},{81,8},{82... | collective-permute-start | bytes 786440 | tf_op jit(solution)/shard_map/ppermute | solution.py:63
  32.3 14.0 %collective-permute-start.6 = (bf16[64,512]{1,0:T(8,128)(2,1)S(1)}, bf16[64,512]{1,0:T(8,128)(2,1)S(1)}, u32[]{:S(2)}, u32[]{:S(2)}) collective-permute-start(bf16[64,512]{1,0:T(8,128)(2,1)S(1)} %get-tuple-element.82), channel_id=1, source_target_pairs={{224,0},{225,1},{226,2},{227,3},{228,4},{229,5},{230,6},{231,7},{2... | collective-permute-start | bytes 196616 | tf_op jit(solution)/shard_map/ppermute | solution.py:63
  37.8 8.5 %collective-permute-start.7 = (bf16[64,512]{1,0:T(8,128)(2,1)S(1)}, bf16[64,512]{1,0:T(8,128)(2,1)S(1)}, u32[]{:S(2)}, u32[]{:S(2)}) collective-permute-start(bf16[64,512]{1,0:T(8,128)(2,1)S(1)} %get-tuple-element.84), channel_id=1, source_target_pairs={{32,0},{33,1},{34,2},{35,3},{36,4},{37,5},{38,6},{39,7},{40,8},{41... | collective-permute-start | bytes 196616 | tf_op jit(solution)/shard_map/ppermute | solution.py:63
  46.8 14.9 %collective-permute-start.11 = (bf16[1024,4,128]{2,1,0:T(4,128)(2,1)S(1)}, bf16[1024,4,128]{2,1,0:T(4,128)(2,1)S(1)}, u32[]{:S(2)}, u32[]{:S(2)}) collective-permute-start(bf16[1024,4,128]{2,1,0:T(4,128)(2,1)S(1)} %constant_dynamic-update-slice_fusion.refs_13_), channel_id=1, source_target_pairs={{64,0},{65,1},{66,2},{67,3},{68,4},{69,5},{70,6},{71,7},{72,8},{73... | collective-permute-start | bytes 3145736 | tf_op jit(solution)/shard_map/ppermute | solution.py:63
  48.0 18.2 %collective-permute-start.13 = (bf16[1024,4,128]{2,1,0:T(4,128)(2,1)S(1)}, bf16[1024,4,128]{2,1,0:T(4,128)(2,1)S(1)}, u32[]{:S(2)}, u32[]{:S(2)}) collective-permute-start(bf16[1024,4,128]{2,1,0:T(4,128)(2,1)S(1)} %constant_dynamic-update-slice_fusion.refs_13_), channel_id=1, source_target_pairs={{1,0},{2,1},{3,2},{4,3},{5,4},{6,5},{7,6},{0,7},{9,8},{10,9},{11,1... | collective-permute-start | bytes 3145736 | tf_op jit(solution)/shard_map/ppermute | solution.py:63
  48.1 18.0 %collective-permute-start.12 = (bf16[1024,4,128]{2,1,0:T(4,128)(2,1)S(1)}, bf16[1024,4,128]{2,1,0:T(4,128)(2,1)S(1)}, u32[]{:S(2)}, u32[]{:S(2)}) collective-permute-start(bf16[1024,4,128]{2,1,0:T(4,128)(2,1)S(1)} %constant_dynamic-update-slice_fusion.refs_13_), channel_id=1, source_target_pairs={{8,0},{9,1},{10,2},{11,3},{12,4},{13,5},{14,6},{15,7},{16,8},{17,9... | collective-permute-start | bytes 3145736 | tf_op jit(solution)/shard_map/ppermute | solution.py:63
  48.2 18.5 %collective-permute-start.14 = (bf16[1024,4,128]{2,1,0:T(4,128)(2,1)S(1)}, bf16[1024,4,128]{2,1,0:T(4,128)(2,1)S(1)}, u32[]{:S(2)}, u32[]{:S(2)}) collective-permute-start(bf16[1024,4,128]{2,1,0:T(4,128)(2,1)S(1)} %constant_dynamic-update-slice_fusion.refs_13_), channel_id=1, source_target_pairs={{32,0},{33,1},{34,2},{35,3},{36,4},{37,5},{38,6},{39,7},{40,8},{41... | collective-permute-start | bytes 3145736 | tf_op jit(solution)/shard_map/ppermute | solution.py:63
  61.7 5.0 %collective-permute-start.15 = (bf16[1024,4,128]{2,1,0:T(4,128)(2,1)S(1)}, bf16[1024,4,128]{2,1,0:T(4,128)(2,1)S(1)}, u32[]{:S(2)}, u32[]{:S(2)}) collective-permute-start(bf16[1024,4,128]{2,1,0:T(4,128)(2,1)S(1)} %collective-permute-done.11.refs_14_), channel_id=1, source_target_pairs={{32,0},{33,1},{34,2},{35,3},{36,4},{37,5},{38,6},{39,7},{40,8},{41... | collective-permute-start | bytes 3145736 | tf_op jit(solution)/shard_map/ppermute | solution.py:63
  66.2 4.9 %collective-permute-start.16 = (bf16[1024,4,128]{2,1,0:T(4,128)(2,1)S(1)}, bf16[1024,4,128]{2,1,0:T(4,128)(2,1)S(1)}, u32[]{:S(2)}, u32[]{:S(2)}) collective-permute-start(bf16[1024,4,128]{2,1,0:T(4,128)(2,1)S(1)} %collective-permute-done.12.refs_15_), channel_id=1, source_target_pairs={{32,0},{33,1},{34,2},{35,3},{36,4},{37,5},{38,6},{39,7},{40,8},{41... | collective-permute-start | bytes 3145736 | tf_op jit(solution)/shard_map/ppermute | solution.py:63
  66.3 4.8 %collective-permute-start.17 = (bf16[1024,4,128]{2,1,0:T(4,128)(2,1)S(1)}, bf16[1024,4,128]{2,1,0:T(4,128)(2,1)S(1)}, u32[]{:S(2)}, u32[]{:S(2)}) collective-permute-start(bf16[1024,4,128]{2,1,0:T(4,128)(2,1)S(1)} %collective-permute-done.13.refs_16_), channel_id=1, source_target_pairs={{32,0},{33,1},{34,2},{35,3},{36,4},{37,5},{38,6},{39,7},{40,8},{41... | collective-permute-start | bytes 3145736 | tf_op jit(solution)/shard_map/ppermute | solution.py:63

commit v2 on v1

--- a/solution.py
+++ b/solution.py
@@ -160,7 +160,8 @@
     def push(b, carry):
         info = far_meta[b].astype(jnp.int32)
         spots = (iota((256, BLOCK), 0) == info[0:1]).astype(BF16)
-        block = dot(place_ref[...], spots)[0:1].astype(jnp.int32)
+        mine = place_ref[pl.ds(pl.multiple_of(spot_ref[3] * 16, 16), 16)]
+        block = dot(mine, spots)[0:1].astype(jnp.int32)
         code_out_ref[b] = block * 32 + info[1:2]
         live = iota((1, BLOCK), 1) + b * BLOCK < total
         rcv_b = jnp.where(live, info[2:3] * 128 + info[3:4], NODE)
@@ -222,7 +223,7 @@
     lax.fori_loop(first, last, gather, 0)
 
 
-def near_kernel(begin, end, pieces, *refs):
+def near_kernel(begin, whole, half, pieces, *refs):
     (
         snd_ref, rcv_ref, edges_ref, tr_ref,
         w_edge_ref, b1_ref, w2_ref, b2_ref, gain_ref, shift_ref,
@@ -267,9 +268,10 @@
         cols = jnp.transpose(both.astype(F32), (1, 0)).astype(jnp.int32)
         return cols[:, 0:1], cols[:, 1:2]
 
-    def step(i, carry):
-        snd = snd_ref[i]
-        rcv = rcv_ref[i]
+    def step(unit, size):
+        units = range(size // SUB)
+        snd = jnp.concatenate([snd_ref[unit + k] for k in units], axis=1)
+        rcv = jnp.concatenate([rcv_ref[unit + k] for k in units], axis=1)
         far = snd >= NEAR
         live = rcv < NODE
         low = jnp.min(rcv)
@@ -283,43 +285,48 @@
             window[:WINDOW] = tr_ref[pl.ds(start, WINDOW)]
             snd_v, rcv_v = columns(snd_n, jnp.where(live, rcv - start, WINDOW + 15))
             parts = []
-            for k in range(0, TILE, SUB):
+            for k in range(0, size, SUB):
                 col = snd_v[k:k + SUB]
                 hot_s = (iota((SUB, NEAR), 1) == col).astype(BF16)
                 hot_r = (iota((SUB, 256), 1) == rcv_v[k:k + SUB]).astype(BF16)
-                at = pl.ds(pl.multiple_of(i * TILE + k, SUB), SUB)
+                at = pl.ds(pl.multiple_of(unit * SUB + k, SUB), SUB)
                 parts.append(edge_rows(at, col, [hot_s, hot_r], [ts_ref[...], window[...]]))
-            hot_n = (iota((WINDOW, TILE), 0) == jnp.where(far, -1, rcv - start)).astype(BF16)
+            hot_n = (iota((WINDOW, size), 0) == jnp.where(far, -1, rcv - start)).astype(BF16)
             agg_ref[pl.ds(start, WINDOW)] += dot(hot_n, jnp.concatenate(parts, axis=0))
 
         @pl.when(jnp.logical_not(narrow))
         def _():
             snd_v, rcv_v = columns(snd_n, jnp.minimum(rcv, NODE - 1))
-            snd_c[...] = snd_v
-            rcv_c[...] = rcv_v
+            snd_c[:size] = snd_v
+            rcv_c[:size] = rcv_v
 
             def some(j, c):
                 at = pl.ds(pl.multiple_of(j * 128, 128), 128)
                 col = snd_c[at]
                 hot_s = (iota((128, NEAR), 1) == col).astype(BF16)
                 hot_r = (iota((128, NODE), 1) == rcv_c[at]).astype(BF16)
-                there = pl.ds(pl.multiple_of(i * TILE + j * 128, 128), 128)
+                there = pl.ds(pl.multiple_of(unit * SUB + j * 128, 128), 128)
                 updates[at] = edge_rows(there, col, [hot_s, hot_r], [ts_ref[...], tr_ref[...]])
                 return c
 
-            lax.fori_loop(0, TILE // 128, some, 0)
+            lax.fori_loop(0, size // 128, some, 0)
 
             def sums(j, c):
                 at = pl.ds(pl.multiple_of(j * 128, 128), 128)
-                hot_n = (iota((128, TILE), 0) + j * 128 == jnp.where(far, -1, rcv)).astype(BF16)
-                agg_ref[at] += dot(hot_n, updates[...])
+                hot_n = (iota((128, size), 0) + j * 128 == jnp.where(far, -1, rcv)).astype(BF16)
+                agg_ref[at] += dot(hot_n, updates[:size])
                 return c
 
             lax.fori_loop(0, NODE // 128, sums, 0)
 
+    def tile(i, carry):
+        step(begin + 2 * i, TILE)
         return carry
 
-    lax.fori_loop(begin, end, step, 0)
+    if whole:
+        lax.fori_loop(0, whole, tile, 0)
+    if half:
+        step(begin + 2 * whole, SUB)
     if begin and pieces:
         for copy in copies:
             copy.wait()
@@ -530,7 +537,7 @@
     )(*args)
 
 
-def near(begin, end, pieces, *args):
+def near(begin, whole, half, pieces, *args):
     outs = [kept((EDGE, D), BF16), kept((NODE, D), F32)]
     scratch = [
         pltpu.VMEM((256, D), BF16), pltpu.VMEM((TILE, 1), jnp.int32), pltpu.VMEM((TILE, 1), jnp.int32),
@@ -542,14 +549,14 @@
         outs = outs + [kept((8192, 4, 128), BF16)]
         scratch = [pltpu.SemaphoreType.DMA((pieces,))] + scratch
     return pl.pallas_call(
-        functools.partial(near_kernel, begin, end, pieces),
+        functools.partial(near_kernel, begin, whole, half, pieces),
         in_specs=[SMEM if k == 10 and begin == 0 else VMEM for k in range(len(args))],
         out_specs=[VMEM] * len(outs),
         out_shape=outs,
         scratch_shapes=scratch,
         input_output_aliases={11: 0, 12: 1} if begin else {},
         compiler_params=pltpu.CompilerParams(vmem_limit_bytes=16 << 20),
-        cost_estimate=pl.CostEstimate(flops=(end - begin) << 31, bytes_accessed=(end - begin) << 21, transcendentals=0),
+        cost_estimate=pl.CostEstimate(flops=(2 * whole + half) << 30, bytes_accessed=(2 * whole + half) << 20, transcendentals=0),
     )(*args)
 
 
@@ -577,15 +584,14 @@
     w_node_self, w_node_aggr, bias_node1, w_node2, bias_node2, gain_node, shift_node,
 ):
     row = lambda v: v.reshape(1, D)
-    tiles = lambda v: v.reshape(TILES, 1, TILE)
+    tiles = lambda v, size: v.reshape(EDGE // size, 1, size)
     after = lambda v, *first: lax.optimization_barrier((v,) + first)[0]
     x, c, y, z = (lax.axis_index(a) for a in AXES)
     spot = jnp.stack([x, y, z, c]).astype(jnp.int32)
     held = nodes[:COARSE_DEV].astype(BF16).reshape(COARSE_DEV, 4, 128)
     nodes, own, *out = pick(spot, nodes, send_rows)
     nodes, own = keep(nodes), keep(own)
-    tables = jnp.asarray(np.repeat(PLACES.reshape(2, 1, 256), 8, axis=1), BF16)
-    place = jnp.where(c == 0, tables[0], tables[1])
+    place = jnp.asarray(np.repeat(PLACES.reshape(2, 256), 16, axis=0), BF16)
 
     def grow(held, stage, *first):
         got = [from_chip(held, pair) for pair in stage]
@@ -594,35 +600,35 @@
     held = after(grow(held, STAGES[0]), own)
     halo = [shift_patch(after(out[0], held), 1), shift_patch(after(out[1], held), -1)]
     names = load(
-        after(edges, held), tiles(sender), tiles(receiver), w_sender, w_edge, w_edge2, w_receiver,
+        after(edges, held), tiles(sender, SUB), tiles(receiver, SUB), tiles(sender, TILE), tiles(receiver, TILE), w_sender, w_edge, w_edge2, w_receiver,
         w_node_self, w_node_aggr, w_node2,
         row(bias_edge1), row(bias_edge2), row(gain_edge), row(shift_edge),
-        row(bias_node1), row(bias_node2), row(gain_node), row(shift_node),
+        row(bias_node1), row(bias_node2), row(gain_node), row(shift_node), place,
     )
     (
-        edges, snd, rcv, w_sender, w_edge, w_edge2, w_receiver, w_node_self, w_node_aggr, w_node2,
-        bias_edge1, *vectors,
+        edges, snd, rcv, snd_t, rcv_t, w_sender, w_edge, w_edge2, w_receiver, w_node_self, w_node_aggr, w_node2,
+        bias_edge1, *vectors, place,
     ) = (keep(v) for v in names)
     edge_vectors, node_vectors = vectors[:3], vectors[3:]
 
-    def edge_part(begin, end, pieces, *extra):
-        outs = near(begin, end, pieces, snd, rcv, edges, tr, w_edge, bias_edge1, w_edge2, *edge_vectors, *extra)
+    def edge_part(begin, whole, half, pieces, *extra):
+        outs = near(begin, whole, half, pieces, snd, rcv, edges, tr, w_edge, bias_edge1, w_edge2, *edge_vectors, *extra)
         return [keep(v) for v in outs]
 
     held = after(grow(held, STAGES[1]), edges, *halo)
     halo = halo + [next_chip(after(out[2], held)), other_core(after(out[3], held))]
     slot, info, far_code, far_rcv, own_ts, tr, far_edges, far_pre = compact(
-        spot, snd, rcv, edges, keep(after(own, held)), w_sender, w_receiver, w_edge, bias_edge1, place,
+        spot, snd_t, rcv_t, edges, keep(after(own, held)), w_sender, w_receiver, w_edge, bias_edge1, place,
     )
     slot, far_rcv, own_ts, tr = (keep(v) for v in (slot, far_rcv, own_ts, tr))
     held = grow(held, STAGES[2], tr, *halo)
     last = [from_chip(held, pair) for pair in LAST]
-    done, agg, ts = edge_part(0, 2, 0, spot, keep(after(own_ts, held)), *halo, w_sender)
+    done, agg, ts = edge_part(0, 2, 1, 0, spot, keep(after(own_ts, held)), *halo, w_sender)
     first = [other_core(held), other_core(after(last[0], agg))]
-    done, agg = edge_part(2, 3, 0, ts, done, agg)
+    done, agg = edge_part(5, 0, 1, 0, ts, done, agg)
     second = [other_core(after(piece, agg)) for piece in last[1:]]
     early = [held, *last, *first]
-    done, agg, table = edge_part(3, 4, 6, ts, done, agg, *early)
+    done, agg, table = edge_part(6, 1, 0, 6, ts, done, agg, *early)
     new_nodes, new_edges, _, _ = far(
         info, far_code, table, *second, done,
         far_away(far_edges), far_away(far_pre), agg, slot, far_rcv, nodes,

time: 82.8 us -> 80.8 us (0.976)
  waiting for transfers between devices: 1.3 us -> 0.05 us
    ppermute x18, waiting for transfers between devices: 1.3 us -> 0.05 us  [receive(): lax.ppermute(block, AXES, [(device(*source(*spot)), device(*spot)) for sp...]
  transfers between devices with their start and end apart: 18 -> 18, of which waited for: 1 -> 0; matrix products, arithmetic and copies ran while one was open for 2% -> 1% of each run, Pallas kernels for 37% -> 38%
where the time goes in v2:
time: 80.8 us; the launch traced here: 80.7 us
  Pallas kernels  42.2 us (52%)
  starting transfers between devices  35.8 us (44%)
  local copies, waits for them, and re-layouts  1.31 us (2%)
  between operations  1.04 us (1%)
    ppermute x18, starting transfers between devices, receive(): lax.ppermute(block, AXES, [(device(*source(*spot)), device(*spot)) for sp...  35.8 us
    pallas_call x3, Pallas kernels, near(): pl.pallas_call(functools.partial(near_kernel, begin, whole, half, pieces)...  16.8 us
    pallas_call x1, Pallas kernels, far(): pl.pallas_call(far_kernel, in_specs=[SMEM] * 2 + [VMEM] + [ANY] * LATE +...  11.2 us
    pallas_call x1, Pallas kernels, compact(): pl.pallas_call(compact_kernel, in_specs=[SMEM] + [VMEM] * (len(args) - 1)...  8.36 us
    pallas_call x1, Pallas kernels, load(): pl.pallas_call(load_kernel, in_specs=[HBM] * count, out_specs=[VMEM] * co...  3.48 us
    pallas_call x1, Pallas kernels, pick(): pl.pallas_call(pick_kernel, in_specs=[SMEM, HBM, HBM], out_specs=[VMEM] *...  2.3 us
  transfers between devices with their start and end apart: 18, of which 0 were waited for; matrix products, arithmetic and copies ran while one was open for 1% of the time, Pallas kernels for 38%

profile of v2, /device:TPU:1, one launch (start us, length us, event | category | flops | bytes accessed | tf_op | source)
XLA Modules:
  0.0 80.7 jit_solution(14256258748382745867)
XLA Ops:
  0.6 0.8 %slice.7 = bf16[32,512]{1,0:T(8,128)(2,1)S(1)} slice(f32[512,512]{1,0:T(8,128)} %nodes_in.1), slice={[0:32], [0:512]} | slice | bytes 65536 | tf_op jit(solution)/shard_map/slice | solution.py:591
  1.5 7.8 %collective-permute-start = (bf16[32,4,128]{2,1,0:T(4,128)(2,1)S(1)}, bf16[32,4,128]{2,1,0:T(4,128)(2,1)S(1)}, u32[]{:S(2)}, u32[]{:S(2)}) collective-permute-start(bf16[32,4,128]{2,1,0:T(4,128)(2,1)S(1)} %reshape.43), channel_id=1, source_target_pairs={{4,0},{5,1},{6,2},{7,3},{0,4},{1,5},{2,6},{3,7},{12,8},{13,9},{14,... | collective-permute-start | bytes 98312 | tf_op jit(solution)/shard_map/ppermute | solution.py:63
  9.3 0.1 pad_add_fusion.spot_ref.refs_10_
  9.4 2.3 %shard_map.212 = (f32[512,512]{1,0:T(8,128)S(1)}, bf16[512,512]{1,0:T(8,128)(2,1)S(1)}, bf16[64,512]{1,0:T(8,128)(2,1)S(1)}, bf16[64,512]{1,0:T(8,128)(2,1)S(1)}...) custom-call(s32[4]{0:T(128)S(1)} %pad_add_fusion.spot_ref.refs_10_, f32[512,512]{1,0:T(8,128)} %nodes_in.1, ...), custom_call_target="tpu_custom_call" | custom-call | flops 134217728 | bytes 2097152 | tf_op jit(solution)/shard_map/pallas_call | solution.py:507
  11.7 0.0 collective-permute-done
  11.8 5.5 %collective-permute-start.3 = (bf16[64,4,128]{2,1,0:T(4,128)(2,1)S(1)}, bf16[64,4,128]{2,1,0:T(4,128)(2,1)S(1)}, u32[]{:S(2)}, u32[]{:S(2)}) collective-permute-start(bf16[64,4,128]{2,1,0:T(4,128)(2,1)S(1)} %pad_maximum_fusion.1), channel_id=1, source_target_pairs={{144,0},{145,1},{146,2},{147,3},{148,4},{149,5},{150,6},{151,7},{1... | collective-permute-start | bytes 196616 | tf_op jit(solution)/shard_map/ppermute | solution.py:63
  17.2 0.2 collective-permute-start.2
  17.5 0.2 collective-permute-start.1
  17.6 0.7 collective-permute-start.4
  18.4 4.6 %collective-permute-start.5 = (bf16[64,512]{1,0:T(8,128)(2,1)S(1)}, bf16[64,512]{1,0:T(8,128)(2,1)S(1)}, u32[]{:S(2)}, u32[]{:S(2)}) collective-permute-start(bf16[64,512]{1,0:T(8,128)(2,1)S(1)} %get-tuple-element.69), channel_id=1, source_target_pairs={{1,0},{2,1},{3,2},{4,3},{5,4},{6,5},{7,6},{8,7},{9,8},{10,9},{11,1... | collective-permute-start | bytes 196616 | tf_op jit(solution)/shard_map/ppermute | solution.py:63
  22.9 3.5 %shard_map.213 = (bf16[4096,512]{1,0:T(8,128)(2,1)S(1)}, s32[8,1,512]{2,1,0:T(1,128)S(1)}, s32[8,1,512]{2,1,0:T(1,128)S(1)}, s32[4,1,1024]{2,1,0:T(1,128)S(1)}, ...) custom-call(bf16[4096,512]{1,0:T(8,128)(2,1)} %refs_0_, ...), custom_call_target="tpu_custom_call" | custom-call | bytes 16777216 | tf_op jit(solution)/shard_map/pallas_call | solution.py:495
  26.4 0.0 collective-permute-done.3
  26.4 0.0 collective-permute-done.2
  26.4 0.0 collective-permute-done.1
  26.5 0.2 pad_maximum_fusion
  26.7 0.0 collective-permute-done.4.refs_12_
  26.7 0.0 collective-permute-done.5.refs_13_
  26.7 0.1 collective-permute-start.10
  26.8 4.8 %collective-permute-start.9 = (bf16[256,4,128]{2,1,0:T(4,128)(2,1)S(1)}, bf16[256,4,128]{2,1,0:T(4,128)(2,1)S(1)}, u32[]{:S(2)}, u32[]{:S(2)}) collective-permute-start(bf16[256,4,128]{2,1,0:T(4,128)(2,1)S(1)} %pad_maximum_fusion), channel_id=1, source_target_pairs={{223,0},{216,1},{217,2},{218,3},{219,4},{220,5},{221,6},{222,7},{1... | collective-permute-start | bytes 786440 | tf_op jit(solution)/shard_map/ppermute | solution.py:63
  31.6 0.0 collective-permute-start.8
  31.6 5.6 %collective-permute-start.6 = (bf16[64,512]{1,0:T(8,128)(2,1)S(1)}, bf16[64,512]{1,0:T(8,128)(2,1)S(1)}, u32[]{:S(2)}, u32[]{:S(2)}) collective-permute-start(bf16[64,512]{1,0:T(8,128)(2,1)S(1)} %get-tuple-element.88), channel_id=1, source_target_pairs={{224,0},{225,1},{226,2},{227,3},{228,4},{229,5},{230,6},{231,7},{2... | collective-permute-start | bytes 196616 | tf_op jit(solution)/shard_map/ppermute | solution.py:63
  37.2 0.1 collective-permute-start.7
  37.3 8.4 %shard_map.214 = (s32[4,1,1024]{2,1,0:T(1,128)S(1)}, s32[16]{0:T(128)S(1)}, s32[18,1,256]{2,1,0:T(1,128)S(1)}, s32[18,1,256]{2,1,0:T(1,128)S(1)}, bf16[512,512]{...) custom-call(s32[4]{0:T(128)S(1)} %pad_add_fusion.spot_ref.refs_10_, ...), custom_call_target="tpu_custom_call" | custom-call | flops 4294967296 | bytes 8388608 | tf_op jit(solution)/shard_map/pallas_call | solution.py:520
  45.6 0.0 collective-permute-done.6.refs_14_
  45.7 0.0 collective-permute-done.7.refs_15_
  45.7 0.1 constant_dynamic-update-slice_fusion.3
  45.8 0.0 collective-permute-done.8
  45.8 0.1 constant_dynamic-update-slice_fusion.2
  45.9 0.0 collective-permute-done.9
  45.9 0.1 constant_dynamic-update-slice_fusion.1
  46.0 0.0 collective-permute-done.10
  46.0 0.1 constant_dynamic-update-slice_fusion.refs_13_
  46.1 1.2 %collective-permute-start.11 = (bf16[1024,4,128]{2,1,0:T(4,128)(2,1)S(1)}, bf16[1024,4,128]{2,1,0:T(4,128)(2,1)S(1)}, u32[]{:S(2)}, u32[]{:S(2)}) collective-permute-start(bf16[1024,4,128]{2,1,0:T(4,128)(2,1)S(1)} %constant_dynamic-update-slice_fusion.refs_13_), channel_id=1, source_target_pairs={{64,0},{65,1},{66,2},{67,3},{68,4},{69,5},{70,6},{71,7},{72,8},{73... | collective-permute-start | bytes 3145736 | tf_op jit(solution)/shard_map/ppermute | solution.py:63
  47.3 0.1 collective-permute-start.13
  47.4 0.1 collective-permute-start.12
  47.5 4.1 %collective-permute-start.14 = (bf16[1024,4,128]{2,1,0:T(4,128)(2,1)S(1)}, bf16[1024,4,128]{2,1,0:T(4,128)(2,1)S(1)}, u32[]{:S(2)}, u32[]{:S(2)}) collective-permute-start(bf16[1024,4,128]{2,1,0:T(4,128)(2,1)S(1)} %constant_dynamic-update-slice_fusion.refs_13_), channel_id=1, source_target_pairs={{32,0},{33,1},{34,2},{35,3},{36,4},{37,5},{38,6},{39,7},{40,8},{41... | collective-permute-start | bytes 3145736 | tf_op jit(solution)/shard_map/ppermute | solution.py:63
  51.6 10.4 %shard_map.215 = (bf16[4096,512]{1,0:T(8,128)(2,1)S(1)}, f32[512,512]{1,0:T(8,128)S(1)}, bf16[768,512]{1,0:T(8,128)(2,1)S(1)}) custom-call(s32[8,1,512]{2,1,0:T(1,128)S(1)} %get-tuple-element.79.refs_0_, s32[8,1,512]{2,1,0:T(1,128)S(1)} %get-tuple-element.80.refs_1_, bf16[4096,512]{1,0:T(8,128)(2,1)S(1)} %get-tuple-element.65.edges_ref.refs_2_, ...), custom_call_target="tpu_custom_call" | custom-call | flops 5368709120 | bytes 5242880 | tf_op jit(solution)/shard_map/pallas_call | solution.py:551
  62.0 0.0 collective-permute-done.11.refs_14_
  62.0 0.1 collective-permute-start.15
  62.1 2.1 %shard_map.216 = (bf16[4096,512]{1,0:T(8,128)(2,1)S(1)}, f32[512,512]{1,0:T(8,128)S(1)}) custom-call(s32[8,1,512]{2,1,0:T(1,128)S(1)} %get-tuple-element.79.refs_0_, s32[8,1,512]{2,1,0:T(1,128)S(1)} %get-tuple-element.80.refs_1_, bf16[4096,512]{1,0:T(8,128)(2,1)S(1)} %get-tuple-element.65.edges_ref.refs_2_, ...), custom_call_target="tpu_custom_call", output_to_operand_aliasing={{0}: (11, {}), {1}: (12, {})} | custom-call | flops 1073741824 | bytes 1048576 | tf_op jit(solution)/shard_map/pallas_call | solution.py:551
  64.3 0.0 collective-permute-done.13.refs_16_
  64.3 0.0 collective-permute-done.12.refs_15_
  64.3 0.6 collective-permute-start.16
  64.9 0.1 collective-permute-start.17
  65.0 0.0 collective-permute-done.14.refs_17_
  65.0 0.0 collective-permute-done.15.refs_18_
  65.0 4.3 %shard_map.217 = (bf16[4096,512]{1,0:T(8,128)(2,1)S(1)}, f32[512,512]{1,0:T(8,128)S(1)}, bf16[8192,4,128]{2,1,0:T(4,128)(2,1)S(1)}) custom-call(s32[8,1,512]{2,1,0:T(1,128)S(1)} %get-tuple-element.79.refs_0_, s32[8,1,512]{2,1,0:T(1,128)S(1)} %get-tuple-element.80.refs_1_, ...), custom_call_target="tpu_custom_call", output_to_operand_aliasing={{0}: (11, {}), {1}: (12, {})} | custom-call | flops 2147483648 | bytes 2097152 | tf_op jit(solution)/shard_map/pallas_call | solution.py:551
  69.3 0.0 collective-permute-done.16.refs_1_
  69.3 0.0 collective-permute-done.17.refs_2_
  69.3 11.2 %shard_map.218 = (f32[512,512]{1,0:T(8,128)}, bf16[4096,512]{1,0:T(8,128)(2,1)}, bf16[8192,4,128]{2,1,0:T(4,128)(2,1)S(1)}, bf16[4096,512]{1,0:T(8,128)(2,1)S(1)}) custom-call(s32[16]{0:T(128)S(1)} %get-tuple-element.77.info_ref, s32[18,1,256]{2,1,0:T(1,128)S(1)} %get-tuple-element.78.code_ref, ...), custom_call_target="tpu_custom_call", output_to_operand_aliasing={{2}: (2, {}), {3}: (5, {})} | custom-call | flops 4294967296 | bytes 25165824 | tf_op jit(solution)/shard_map/pallas_call | solution.py:564
  (2 shorter events, 0.1 us)
Async XLA Ops:
  1.5 10.2 %collective-permute-start = (bf16[32,4,128]{2,1,0:T(4,128)(2,1)S(1)}, bf16[32,4,128]{2,1,0:T(4,128)(2,1)S(1)}, u32[]{:S(2)}, u32[]{:S(2)}) collective-permute-start(bf16[32,4,128]{2,1,0:T(4,128)(2,1)S(1)} %reshape.43), channel_id=1, source_target_pairs={{4,0},{5,1},{6,2},{7,3},{0,4},{1,5},{2,6},{3,7},{12,8},{13,9},{14,... | collective-permute-start | bytes 98312 | tf_op jit(solution)/shard_map/ppermute | solution.py:63
  11.8 14.7 %collective-permute-start.3 = (bf16[64,4,128]{2,1,0:T(4,128)(2,1)S(1)}, bf16[64,4,128]{2,1,0:T(4,128)(2,1)S(1)}, u32[]{:S(2)}, u32[]{:S(2)}) collective-permute-start(bf16[64,4,128]{2,1,0:T(4,128)(2,1)S(1)} %pad_maximum_fusion.1), channel_id=1, source_target_pairs={{144,0},{145,1},{146,2},{147,3},{148,4},{149,5},{150,6},{151,7},{1... | collective-permute-start | bytes 196616 | tf_op jit(solution)/shard_map/ppermute | solution.py:63
  17.2 9.2 %collective-permute-start.2 = (bf16[64,4,128]{2,1,0:T(4,128)(2,1)S(1)}, bf16[64,4,128]{2,1,0:T(4,128)(2,1)S(1)}, u32[]{:S(2)}, u32[]{:S(2)}) collective-permute-start(bf16[64,4,128]{2,1,0:T(4,128)(2,1)S(1)} %pad_maximum_fusion.1), channel_id=1, source_target_pairs={{16,0},{17,1},{18,2},{19,3},{20,4},{21,5},{22,6},{23,7},{24,8},{25... | collective-permute-start | bytes 196616 | tf_op jit(solution)/shard_map/ppermute | solution.py:63
  17.5 9.0 %collective-permute-start.1 = (bf16[64,4,128]{2,1,0:T(4,128)(2,1)S(1)}, bf16[64,4,128]{2,1,0:T(4,128)(2,1)S(1)}, u32[]{:S(2)}, u32[]{:S(2)}) collective-permute-start(bf16[64,4,128]{2,1,0:T(4,128)(2,1)S(1)} %pad_maximum_fusion.1), channel_id=1, source_target_pairs={{128,0},{129,1},{130,2},{131,3},{132,4},{133,5},{134,6},{135,7},{1... | collective-permute-start | bytes 196616 | tf_op jit(solution)/shard_map/ppermute | solution.py:63
  17.6 9.1 %collective-permute-start.4 = (bf16[64,512]{1,0:T(8,128)(2,1)S(1)}, bf16[64,512]{1,0:T(8,128)(2,1)S(1)}, u32[]{:S(2)}, u32[]{:S(2)}) collective-permute-start(bf16[64,512]{1,0:T(8,128)(2,1)S(1)} %get-tuple-element.67), channel_id=1, source_target_pairs={{31,0},{0,1},{1,2},{2,3},{3,4},{4,5},{5,6},{6,7},{7,8},{8,9},{9,10... | collective-permute-start | bytes 196616 | tf_op jit(solution)/shard_map/ppermute | solution.py:63
  18.4 8.3 %collective-permute-start.5 = (bf16[64,512]{1,0:T(8,128)(2,1)S(1)}, bf16[64,512]{1,0:T(8,128)(2,1)S(1)}, u32[]{:S(2)}, u32[]{:S(2)}) collective-permute-start(bf16[64,512]{1,0:T(8,128)(2,1)S(1)} %get-tuple-element.69), channel_id=1, source_target_pairs={{1,0},{2,1},{3,2},{4,3},{5,4},{6,5},{7,6},{8,7},{9,8},{10,9},{11,1... | collective-permute-start | bytes 196616 | tf_op jit(solution)/shard_map/ppermute | solution.py:63
  26.7 19.3 %collective-permute-start.10 = (bf16[256,4,128]{2,1,0:T(4,128)(2,1)S(1)}, bf16[256,4,128]{2,1,0:T(4,128)(2,1)S(1)}, u32[]{:S(2)}, u32[]{:S(2)}) collective-permute-start(bf16[256,4,128]{2,1,0:T(4,128)(2,1)S(1)} %pad_maximum_fusion), channel_id=1, source_target_pairs={{2,0},{3,1},{4,2},{5,3},{6,4},{7,5},{0,6},{1,7},{10,8},{11,9},{12,... | collective-permute-start | bytes 786440 | tf_op jit(solution)/shard_map/ppermute | solution.py:63
  26.8 19.1 %collective-permute-start.9 = (bf16[256,4,128]{2,1,0:T(4,128)(2,1)S(1)}, bf16[256,4,128]{2,1,0:T(4,128)(2,1)S(1)}, u32[]{:S(2)}, u32[]{:S(2)}) collective-permute-start(bf16[256,4,128]{2,1,0:T(4,128)(2,1)S(1)} %pad_maximum_fusion), channel_id=1, source_target_pairs={{223,0},{216,1},{217,2},{218,3},{219,4},{220,5},{221,6},{222,7},{1... | collective-permute-start | bytes 786440 | tf_op jit(solution)/shard_map/ppermute | solution.py:63
  31.6 14.2 %collective-permute-start.8 = (bf16[256,4,128]{2,1,0:T(4,128)(2,1)S(1)}, bf16[256,4,128]{2,1,0:T(4,128)(2,1)S(1)}, u32[]{:S(2)}, u32[]{:S(2)}) collective-permute-start(bf16[256,4,128]{2,1,0:T(4,128)(2,1)S(1)} %pad_maximum_fusion), channel_id=1, source_target_pairs={{73,0},{74,1},{75,2},{76,3},{77,4},{78,5},{79,6},{72,7},{81,8},{82... | collective-permute-start | bytes 786440 | tf_op jit(solution)/shard_map/ppermute | solution.py:63
  31.6 14.1 %collective-permute-start.6 = (bf16[64,512]{1,0:T(8,128)(2,1)S(1)}, bf16[64,512]{1,0:T(8,128)(2,1)S(1)}, u32[]{:S(2)}, u32[]{:S(2)}) collective-permute-start(bf16[64,512]{1,0:T(8,128)(2,1)S(1)} %get-tuple-element.88), channel_id=1, source_target_pairs={{224,0},{225,1},{226,2},{227,3},{228,4},{229,5},{230,6},{231,7},{2... | collective-permute-start | bytes 196616 | tf_op jit(solution)/shard_map/ppermute | solution.py:63
  37.2 8.5 %collective-permute-start.7 = (bf16[64,512]{1,0:T(8,128)(2,1)S(1)}, bf16[64,512]{1,0:T(8,128)(2,1)S(1)}, u32[]{:S(2)}, u32[]{:S(2)}) collective-permute-start(bf16[64,512]{1,0:T(8,128)(2,1)S(1)} %get-tuple-element.90), channel_id=1, source_target_pairs={{32,0},{33,1},{34,2},{35,3},{36,4},{37,5},{38,6},{39,7},{40,8},{41... | collective-permute-start | bytes 196616 | tf_op jit(solution)/shard_map/ppermute | solution.py:63
  46.1 15.9 %collective-permute-start.11 = (bf16[1024,4,128]{2,1,0:T(4,128)(2,1)S(1)}, bf16[1024,4,128]{2,1,0:T(4,128)(2,1)S(1)}, u32[]{:S(2)}, u32[]{:S(2)}) collective-permute-start(bf16[1024,4,128]{2,1,0:T(4,128)(2,1)S(1)} %constant_dynamic-update-slice_fusion.refs_13_), channel_id=1, source_target_pairs={{64,0},{65,1},{66,2},{67,3},{68,4},{69,5},{70,6},{71,7},{72,8},{73... | collective-permute-start | bytes 3145736 | tf_op jit(solution)/shard_map/ppermute | solution.py:63
  47.3 17.0 %collective-permute-start.13 = (bf16[1024,4,128]{2,1,0:T(4,128)(2,1)S(1)}, bf16[1024,4,128]{2,1,0:T(4,128)(2,1)S(1)}, u32[]{:S(2)}, u32[]{:S(2)}) collective-permute-start(bf16[1024,4,128]{2,1,0:T(4,128)(2,1)S(1)} %constant_dynamic-update-slice_fusion.refs_13_), channel_id=1, source_target_pairs={{1,0},{2,1},{3,2},{4,3},{5,4},{6,5},{7,6},{0,7},{9,8},{10,9},{11,1... | collective-permute-start | bytes 3145736 | tf_op jit(solution)/shard_map/ppermute | solution.py:63
  47.4 16.9 %collective-permute-start.12 = (bf16[1024,4,128]{2,1,0:T(4,128)(2,1)S(1)}, bf16[1024,4,128]{2,1,0:T(4,128)(2,1)S(1)}, u32[]{:S(2)}, u32[]{:S(2)}) collective-permute-start(bf16[1024,4,128]{2,1,0:T(4,128)(2,1)S(1)} %constant_dynamic-update-slice_fusion.refs_13_), channel_id=1, source_target_pairs={{8,0},{9,1},{10,2},{11,3},{12,4},{13,5},{14,6},{15,7},{16,8},{17,9... | collective-permute-start | bytes 3145736 | tf_op jit(solution)/shard_map/ppermute | solution.py:63
  47.5 17.5 %collective-permute-start.14 = (bf16[1024,4,128]{2,1,0:T(4,128)(2,1)S(1)}, bf16[1024,4,128]{2,1,0:T(4,128)(2,1)S(1)}, u32[]{:S(2)}, u32[]{:S(2)}) collective-permute-start(bf16[1024,4,128]{2,1,0:T(4,128)(2,1)S(1)} %constant_dynamic-update-slice_fusion.refs_13_), channel_id=1, source_target_pairs={{32,0},{33,1},{34,2},{35,3},{36,4},{37,5},{38,6},{39,7},{40,8},{41... | collective-permute-start | bytes 3145736 | tf_op jit(solution)/shard_map/ppermute | solution.py:63
  62.0 3.0 %collective-permute-start.15 = (bf16[1024,4,128]{2,1,0:T(4,128)(2,1)S(1)}, bf16[1024,4,128]{2,1,0:T(4,128)(2,1)S(1)}, u32[]{:S(2)}, u32[]{:S(2)}) collective-permute-start(bf16[1024,4,128]{2,1,0:T(4,128)(2,1)S(1)} %collective-permute-done.11.refs_14_), channel_id=1, source_target_pairs={{32,0},{33,1},{34,2},{35,3},{36,4},{37,5},{38,6},{39,7},{40,8},{41... | collective-permute-start | bytes 3145736 | tf_op jit(solution)/shard_map/ppermute | solution.py:63
  64.3 5.0 %collective-permute-start.16 = (bf16[1024,4,128]{2,1,0:T(4,128)(2,1)S(1)}, bf16[1024,4,128]{2,1,0:T(4,128)(2,1)S(1)}, u32[]{:S(2)}, u32[]{:S(2)}) collective-permute-start(bf16[1024,4,128]{2,1,0:T(4,128)(2,1)S(1)} %collective-permute-done.12.refs_15_), channel_id=1, source_target_pairs={{32,0},{33,1},{34,2},{35,3},{36,4},{37,5},{38,6},{39,7},{40,8},{41... | collective-permute-start | bytes 3145736 | tf_op jit(solution)/shard_map/ppermute | solution.py:63
  64.9 4.4 %collective-permute-start.17 = (bf16[1024,4,128]{2,1,0:T(4,128)(2,1)S(1)}, bf16[1024,4,128]{2,1,0:T(4,128)(2,1)S(1)}, u32[]{:S(2)}, u32[]{:S(2)}) collective-permute-start(bf16[1024,4,128]{2,1,0:T(4,128)(2,1)S(1)} %collective-permute-done.13.refs_16_), channel_id=1, source_target_pairs={{32,0},{33,1},{34,2},{35,3},{36,4},{37,5},{38,6},{39,7},{40,8},{41... | collective-permute-start | bytes 3145736 | tf_op jit(solution)/shard_map/ppermute | solution.py:63

commit v3 on v2

--- a/solution.py
+++ b/solution.py
@@ -386,21 +386,19 @@
         lax.fori_loop(0, count // 16, gather, 0)
         for copy in block_copies(b):
             copy.wait()
-        for k in range(SLOTS // BLOCK):
-            here = slice(k * BLOCK, (k + 1) * BLOCK)
-            first = b * SLOTS + k * BLOCK
-            valid = iota((BLOCK, 1), 0) + first < total
-            sent = jnp.concatenate(
-                [rows_buf[pl.ds(k * BLOCK * 4 + c, BLOCK, stride=4)] for c in range(4)], axis=1
-            ).astype(BF16)
-            pre = pre_buf[here] + dot(sent, w_sender[...])
-            hidden = silu(pre).astype(BF16)
-            update = layer_norm(dot(hidden, w2[...]) + b2_ref[...], gain_ref[...], shift_ref[...])
-            update = jnp.where(valid, update, 0.0)
-            new = jnp.where(valid, edges_buf[here].astype(F32) + update, 0.0)
-            new_far[pl.ds(pl.multiple_of(first, BLOCK), BLOCK)] = new.astype(BF16)
-            hot = (iota((NODE, BLOCK), 0) == rcv_ref[b * (SLOTS // BLOCK) + k]).astype(BF16)
-            agg[...] += dot(hot, update.astype(BF16))
+        valid = iota((SLOTS, 1), 0) + b * SLOTS < total
+        sent = jnp.concatenate(
+            [rows_buf[pl.ds(c, SLOTS, stride=4)] for c in range(4)], axis=1
+        ).astype(BF16)
+        pre = pre_buf[...] + dot(sent, w_sender[...])
+        hidden = silu(pre).astype(BF16)
+        update = layer_norm(dot(hidden, w2[...]) + b2_ref[...], gain_ref[...], shift_ref[...])
+        update = jnp.where(valid, update, 0.0)
+        new = jnp.where(valid, edges_buf[...].astype(F32) + update, 0.0)
+        new_far[pl.ds(pl.multiple_of(b * SLOTS, SLOTS), SLOTS)] = new.astype(BF16)
+        receivers = jnp.concatenate([rcv_ref[row + k] for k in range(SLOTS // BLOCK)], axis=1)
+        hot = (iota((NODE, SLOTS), 0) == receivers).astype(BF16)
+        agg[...] += dot(hot, update.astype(BF16))
         return carry
 
     blocks = (total + SLOTS - 1) // SLOTS

time: 80.8 us -> 80.1 us (level)
  transfers between devices with their start and end apart: 18 -> 18, of which waited for: 0 -> 0; matrix products, arithmetic and copies ran while one was open for 1% -> 1% of each run, Pallas kernels for 38% -> 39%
where the time goes in v3:
time: 80.1 us; the launch traced here: 79.9 us
  Pallas kernels  41.4 us (52%)
  starting transfers between devices  35.8 us (45%)
  local copies, waits for them, and re-layouts  1.31 us (2%)
  between operations  1.04 us (1%)
    ppermute x18, starting transfers between devices, receive(): lax.ppermute(block, AXES, [(device(*source(*spot)), device(*spot)) for sp...  35.8 us
    pallas_call x3, Pallas kernels, near(): pl.pallas_call(functools.partial(near_kernel, begin, whole, half, pieces)...  16.8 us
    pallas_call x1, Pallas kernels, far(): pl.pallas_call(far_kernel, in_specs=[SMEM] * 2 + [VMEM] + [ANY] * LATE +...  10.4 us
    pallas_call x1, Pallas kernels, compact(): pl.pallas_call(compact_kernel, in_specs=[SMEM] + [VMEM] * (len(args) - 1)...  8.36 us
    pallas_call x1, Pallas kernels, load(): pl.pallas_call(load_kernel, in_specs=[HBM] * count, out_specs=[VMEM] * co...  3.48 us
    pallas_call x1, Pallas kernels, pick(): pl.pallas_call(pick_kernel, in_specs=[SMEM, HBM, HBM], out_specs=[VMEM] *...  2.3 us
  transfers between devices with their start and end apart: 18, of which 0 were waited for; matrix products, arithmetic and copies ran while one was open for 1% of the time, Pallas kernels for 39%

profile of v3, /device:TPU:1, one launch (start us, length us, event | category | flops | bytes accessed | tf_op | source)
XLA Modules:
  0.0 79.9 jit_solution(17159904667475774025)
XLA Ops:
  0.6 0.8 %slice.7 = bf16[32,512]{1,0:T(8,128)(2,1)S(1)} slice(f32[512,512]{1,0:T(8,128)} %nodes_in.1), slice={[0:32], [0:512]} | slice | bytes 65536 | tf_op jit(solution)/shard_map/slice | solution.py:589
  1.5 7.8 %collective-permute-start = (bf16[32,4,128]{2,1,0:T(4,128)(2,1)S(1)}, bf16[32,4,128]{2,1,0:T(4,128)(2,1)S(1)}, u32[]{:S(2)}, u32[]{:S(2)}) collective-permute-start(bf16[32,4,128]{2,1,0:T(4,128)(2,1)S(1)} %reshape.43), channel_id=1, source_target_pairs={{4,0},{5,1},{6,2},{7,3},{0,4},{1,5},{2,6},{3,7},{12,8},{13,9},{14,... | collective-permute-start | bytes 98312 | tf_op jit(solution)/shard_map/ppermute | solution.py:63
  9.3 0.1 pad_add_fusion.spot_ref.refs_10_
  9.4 2.3 %shard_map.212 = (f32[512,512]{1,0:T(8,128)S(1)}, bf16[512,512]{1,0:T(8,128)(2,1)S(1)}, bf16[64,512]{1,0:T(8,128)(2,1)S(1)}, bf16[64,512]{1,0:T(8,128)(2,1)S(1)}...) custom-call(s32[4]{0:T(128)S(1)} %pad_add_fusion.spot_ref.refs_10_, f32[512,512]{1,0:T(8,128)} %nodes_in.1, ...), custom_call_target="tpu_custom_call" | custom-call | flops 134217728 | bytes 2097152 | tf_op jit(solution)/shard_map/pallas_call | solution.py:505
  11.7 0.0 collective-permute-done
  11.8 5.5 %collective-permute-start.3 = (bf16[64,4,128]{2,1,0:T(4,128)(2,1)S(1)}, bf16[64,4,128]{2,1,0:T(4,128)(2,1)S(1)}, u32[]{:S(2)}, u32[]{:S(2)}) collective-permute-start(bf16[64,4,128]{2,1,0:T(4,128)(2,1)S(1)} %pad_maximum_fusion.1), channel_id=1, source_target_pairs={{144,0},{145,1},{146,2},{147,3},{148,4},{149,5},{150,6},{151,7},{1... | collective-permute-start | bytes 196616 | tf_op jit(solution)/shard_map/ppermute | solution.py:63
  17.2 0.2 collective-permute-start.2
  17.5 0.2 collective-permute-start.1
  17.6 0.7 collective-permute-start.4
  18.4 4.6 %collective-permute-start.5 = (bf16[64,512]{1,0:T(8,128)(2,1)S(1)}, bf16[64,512]{1,0:T(8,128)(2,1)S(1)}, u32[]{:S(2)}, u32[]{:S(2)}) collective-permute-start(bf16[64,512]{1,0:T(8,128)(2,1)S(1)} %get-tuple-element.69), channel_id=1, source_target_pairs={{1,0},{2,1},{3,2},{4,3},{5,4},{6,5},{7,6},{8,7},{9,8},{10,9},{11,1... | collective-permute-start | bytes 196616 | tf_op jit(solution)/shard_map/ppermute | solution.py:63
  22.9 3.5 %shard_map.213 = (bf16[4096,512]{1,0:T(8,128)(2,1)S(1)}, s32[8,1,512]{2,1,0:T(1,128)S(1)}, s32[8,1,512]{2,1,0:T(1,128)S(1)}, s32[4,1,1024]{2,1,0:T(1,128)S(1)}, ...) custom-call(bf16[4096,512]{1,0:T(8,128)(2,1)} %refs_0_, ...), custom_call_target="tpu_custom_call" | custom-call | bytes 16777216 | tf_op jit(solution)/shard_map/pallas_call | solution.py:493
  26.4 0.0 collective-permute-done.3
  26.4 0.0 collective-permute-done.2
  26.4 0.0 collective-permute-done.1
  26.5 0.2 pad_maximum_fusion
  26.7 0.0 collective-permute-done.4.refs_12_
  26.7 0.0 collective-permute-done.5.refs_13_
  26.7 0.1 collective-permute-start.10
  26.8 4.8 %collective-permute-start.9 = (bf16[256,4,128]{2,1,0:T(4,128)(2,1)S(1)}, bf16[256,4,128]{2,1,0:T(4,128)(2,1)S(1)}, u32[]{:S(2)}, u32[]{:S(2)}) collective-permute-start(bf16[256,4,128]{2,1,0:T(4,128)(2,1)S(1)} %pad_maximum_fusion), channel_id=1, source_target_pairs={{223,0},{216,1},{217,2},{218,3},{219,4},{220,5},{221,6},{222,7},{1... | collective-permute-start | bytes 786440 | tf_op jit(solution)/shard_map/ppermute | solution.py:63
  31.6 0.0 collective-permute-start.8
  31.6 5.6 %collective-permute-start.6 = (bf16[64,512]{1,0:T(8,128)(2,1)S(1)}, bf16[64,512]{1,0:T(8,128)(2,1)S(1)}, u32[]{:S(2)}, u32[]{:S(2)}) collective-permute-start(bf16[64,512]{1,0:T(8,128)(2,1)S(1)} %get-tuple-element.88), channel_id=1, source_target_pairs={{224,0},{225,1},{226,2},{227,3},{228,4},{229,5},{230,6},{231,7},{2... | collective-permute-start | bytes 196616 | tf_op jit(solution)/shard_map/ppermute | solution.py:63
  37.2 0.1 collective-permute-start.7
  37.3 8.4 %shard_map.214 = (s32[4,1,1024]{2,1,0:T(1,128)S(1)}, s32[16]{0:T(128)S(1)}, s32[18,1,256]{2,1,0:T(1,128)S(1)}, s32[18,1,256]{2,1,0:T(1,128)S(1)}, bf16[512,512]{...) custom-call(s32[4]{0:T(128)S(1)} %pad_add_fusion.spot_ref.refs_10_, ...), custom_call_target="tpu_custom_call" | custom-call | flops 4294967296 | bytes 8388608 | tf_op jit(solution)/shard_map/pallas_call | solution.py:518
  45.6 0.0 collective-permute-done.6.refs_14_
  45.7 0.0 collective-permute-done.7.refs_15_
  45.7 0.1 constant_dynamic-update-slice_fusion.3
  45.8 0.0 collective-permute-done.8
  45.8 0.1 constant_dynamic-update-slice_fusion.2
  45.9 0.0 collective-permute-done.9
  45.9 0.1 constant_dynamic-update-slice_fusion.1
  46.0 0.0 collective-permute-done.10
  46.0 0.1 constant_dynamic-update-slice_fusion.refs_13_
  46.1 1.2 %collective-permute-start.11 = (bf16[1024,4,128]{2,1,0:T(4,128)(2,1)S(1)}, bf16[1024,4,128]{2,1,0:T(4,128)(2,1)S(1)}, u32[]{:S(2)}, u32[]{:S(2)}) collective-permute-start(bf16[1024,4,128]{2,1,0:T(4,128)(2,1)S(1)} %constant_dynamic-update-slice_fusion.refs_13_), channel_id=1, source_target_pairs={{64,0},{65,1},{66,2},{67,3},{68,4},{69,5},{70,6},{71,7},{72,8},{73... | collective-permute-start | bytes 3145736 | tf_op jit(solution)/shard_map/ppermute | solution.py:63
  47.3 0.1 collective-permute-start.13
  47.4 0.1 collective-permute-start.12
  47.5 4.1 %collective-permute-start.14 = (bf16[1024,4,128]{2,1,0:T(4,128)(2,1)S(1)}, bf16[1024,4,128]{2,1,0:T(4,128)(2,1)S(1)}, u32[]{:S(2)}, u32[]{:S(2)}) collective-permute-start(bf16[1024,4,128]{2,1,0:T(4,128)(2,1)S(1)} %constant_dynamic-update-slice_fusion.refs_13_), channel_id=1, source_target_pairs={{32,0},{33,1},{34,2},{35,3},{36,4},{37,5},{38,6},{39,7},{40,8},{41... | collective-permute-start | bytes 3145736 | tf_op jit(solution)/shard_map/ppermute | solution.py:63
  51.6 10.4 %shard_map.215 = (bf16[4096,512]{1,0:T(8,128)(2,1)S(1)}, f32[512,512]{1,0:T(8,128)S(1)}, bf16[768,512]{1,0:T(8,128)(2,1)S(1)}) custom-call(s32[8,1,512]{2,1,0:T(1,128)S(1)} %get-tuple-element.79.refs_0_, s32[8,1,512]{2,1,0:T(1,128)S(1)} %get-tuple-element.80.refs_1_, bf16[4096,512]{1,0:T(8,128)(2,1)S(1)} %get-tuple-element.65.edges_ref.refs_2_, ...), custom_call_target="tpu_custom_call" | custom-call | flops 5368709120 | bytes 5242880 | tf_op jit(solution)/shard_map/pallas_call | solution.py:549
  62.0 0.0 collective-permute-done.11.refs_14_
  62.0 0.1 collective-permute-start.15
  62.1 2.1 %shard_map.216 = (bf16[4096,512]{1,0:T(8,128)(2,1)S(1)}, f32[512,512]{1,0:T(8,128)S(1)}) custom-call(s32[8,1,512]{2,1,0:T(1,128)S(1)} %get-tuple-element.79.refs_0_, s32[8,1,512]{2,1,0:T(1,128)S(1)} %get-tuple-element.80.refs_1_, bf16[4096,512]{1,0:T(8,128)(2,1)S(1)} %get-tuple-element.65.edges_ref.refs_2_, ...), custom_call_target="tpu_custom_call", output_to_operand_aliasing={{0}: (11, {}), {1}: (12, {})} | custom-call | flops 1073741824 | bytes 1048576 | tf_op jit(solution)/shard_map/pallas_call | solution.py:549
  64.3 0.0 collective-permute-done.13.refs_16_
  64.3 0.0 collective-permute-done.12.refs_15_
  64.3 0.6 collective-permute-start.16
  64.9 0.1 collective-permute-start.17
  65.0 0.0 collective-permute-done.14.refs_17_
  65.0 0.0 collective-permute-done.15.refs_18_
  65.0 4.3 %shard_map.217 = (bf16[4096,512]{1,0:T(8,128)(2,1)S(1)}, f32[512,512]{1,0:T(8,128)S(1)}, bf16[8192,4,128]{2,1,0:T(4,128)(2,1)S(1)}) custom-call(s32[8,1,512]{2,1,0:T(1,128)S(1)} %get-tuple-element.79.refs_0_, s32[8,1,512]{2,1,0:T(1,128)S(1)} %get-tuple-element.80.refs_1_, ...), custom_call_target="tpu_custom_call", output_to_operand_aliasing={{0}: (11, {}), {1}: (12, {})} | custom-call | flops 2147483648 | bytes 2097152 | tf_op jit(solution)/shard_map/pallas_call | solution.py:549
  69.3 0.0 collective-permute-done.16.refs_1_
  69.3 0.0 collective-permute-done.17.refs_2_
  69.3 10.4 %shard_map.218 = (f32[512,512]{1,0:T(8,128)}, bf16[4096,512]{1,0:T(8,128)(2,1)}, bf16[8192,4,128]{2,1,0:T(4,128)(2,1)S(1)}, bf16[4096,512]{1,0:T(8,128)(2,1)S(1)}) custom-call(s32[16]{0:T(128)S(1)} %get-tuple-element.77.info_ref, s32[18,1,256]{2,1,0:T(1,128)S(1)} %get-tuple-element.78.code_ref, ...), custom_call_target="tpu_custom_call", output_to_operand_aliasing={{2}: (2, {}), {3}: (5, {})} | custom-call | flops 4294967296 | bytes 25165824 | tf_op jit(solution)/shard_map/pallas_call | solution.py:562
  (2 shorter events, 0.1 us)
Async XLA Ops:
  1.5 10.2 %collective-permute-start = (bf16[32,4,128]{2,1,0:T(4,128)(2,1)S(1)}, bf16[32,4,128]{2,1,0:T(4,128)(2,1)S(1)}, u32[]{:S(2)}, u32[]{:S(2)}) collective-permute-start(bf16[32,4,128]{2,1,0:T(4,128)(2,1)S(1)} %reshape.43), channel_id=1, source_target_pairs={{4,0},{5,1},{6,2},{7,3},{0,4},{1,5},{2,6},{3,7},{12,8},{13,9},{14,... | collective-permute-start | bytes 98312 | tf_op jit(solution)/shard_map/ppermute | solution.py:63
  11.8 14.7 %collective-permute-start.3 = (bf16[64,4,128]{2,1,0:T(4,128)(2,1)S(1)}, bf16[64,4,128]{2,1,0:T(4,128)(2,1)S(1)}, u32[]{:S(2)}, u32[]{:S(2)}) collective-permute-start(bf16[64,4,128]{2,1,0:T(4,128)(2,1)S(1)} %pad_maximum_fusion.1), channel_id=1, source_target_pairs={{144,0},{145,1},{146,2},{147,3},{148,4},{149,5},{150,6},{151,7},{1... | collective-permute-start | bytes 196616 | tf_op jit(solution)/shard_map/ppermute | solution.py:63
  17.2 9.2 %collective-permute-start.2 = (bf16[64,4,128]{2,1,0:T(4,128)(2,1)S(1)}, bf16[64,4,128]{2,1,0:T(4,128)(2,1)S(1)}, u32[]{:S(2)}, u32[]{:S(2)}) collective-permute-start(bf16[64,4,128]{2,1,0:T(4,128)(2,1)S(1)} %pad_maximum_fusion.1), channel_id=1, source_target_pairs={{16,0},{17,1},{18,2},{19,3},{20,4},{21,5},{22,6},{23,7},{24,8},{25... | collective-permute-start | bytes 196616 | tf_op jit(solution)/shard_map/ppermute | solution.py:63
  17.5 9.0 %collective-permute-start.1 = (bf16[64,4,128]{2,1,0:T(4,128)(2,1)S(1)}, bf16[64,4,128]{2,1,0:T(4,128)(2,1)S(1)}, u32[]{:S(2)}, u32[]{:S(2)}) collective-permute-start(bf16[64,4,128]{2,1,0:T(4,128)(2,1)S(1)} %pad_maximum_fusion.1), channel_id=1, source_target_pairs={{128,0},{129,1},{130,2},{131,3},{132,4},{133,5},{134,6},{135,7},{1... | collective-permute-start | bytes 196616 | tf_op jit(solution)/shard_map/ppermute | solution.py:63
  17.6 9.1 %collective-permute-start.4 = (bf16[64,512]{1,0:T(8,128)(2,1)S(1)}, bf16[64,512]{1,0:T(8,128)(2,1)S(1)}, u32[]{:S(2)}, u32[]{:S(2)}) collective-permute-start(bf16[64,512]{1,0:T(8,128)(2,1)S(1)} %get-tuple-element.67), channel_id=1, source_target_pairs={{31,0},{0,1},{1,2},{2,3},{3,4},{4,5},{5,6},{6,7},{7,8},{8,9},{9,10... | collective-permute-start | bytes 196616 | tf_op jit(solution)/shard_map/ppermute | solution.py:63
  18.4 8.3 %collective-permute-start.5 = (bf16[64,512]{1,0:T(8,128)(2,1)S(1)}, bf16[64,512]{1,0:T(8,128)(2,1)S(1)}, u32[]{:S(2)}, u32[]{:S(2)}) collective-permute-start(bf16[64,512]{1,0:T(8,128)(2,1)S(1)} %get-tuple-element.69), channel_id=1, source_target_pairs={{1,0},{2,1},{3,2},{4,3},{5,4},{6,5},{7,6},{8,7},{9,8},{10,9},{11,1... | collective-permute-start | bytes 196616 | tf_op jit(solution)/shard_map/ppermute | solution.py:63
  26.7 19.3 %collective-permute-start.10 = (bf16[256,4,128]{2,1,0:T(4,128)(2,1)S(1)}, bf16[256,4,128]{2,1,0:T(4,128)(2,1)S(1)}, u32[]{:S(2)}, u32[]{:S(2)}) collective-permute-start(bf16[256,4,128]{2,1,0:T(4,128)(2,1)S(1)} %pad_maximum_fusion), channel_id=1, source_target_pairs={{2,0},{3,1},{4,2},{5,3},{6,4},{7,5},{0,6},{1,7},{10,8},{11,9},{12,... | collective-permute-start | bytes 786440 | tf_op jit(solution)/shard_map/ppermute | solution.py:63
  26.8 19.1 %collective-permute-start.9 = (bf16[256,4,128]{2,1,0:T(4,128)(2,1)S(1)}, bf16[256,4,128]{2,1,0:T(4,128)(2,1)S(1)}, u32[]{:S(2)}, u32[]{:S(2)}) collective-permute-start(bf16[256,4,128]{2,1,0:T(4,128)(2,1)S(1)} %pad_maximum_fusion), channel_id=1, source_target_pairs={{223,0},{216,1},{217,2},{218,3},{219,4},{220,5},{221,6},{222,7},{1... | collective-permute-start | bytes 786440 | tf_op jit(solution)/shard_map/ppermute | solution.py:63
  31.6 14.2 %collective-permute-start.8 = (bf16[256,4,128]{2,1,0:T(4,128)(2,1)S(1)}, bf16[256,4,128]{2,1,0:T(4,128)(2,1)S(1)}, u32[]{:S(2)}, u32[]{:S(2)}) collective-permute-start(bf16[256,4,128]{2,1,0:T(4,128)(2,1)S(1)} %pad_maximum_fusion), channel_id=1, source_target_pairs={{73,0},{74,1},{75,2},{76,3},{77,4},{78,5},{79,6},{72,7},{81,8},{82... | collective-permute-start | bytes 786440 | tf_op jit(solution)/shard_map/ppermute | solution.py:63
  31.6 14.1 %collective-permute-start.6 = (bf16[64,512]{1,0:T(8,128)(2,1)S(1)}, bf16[64,512]{1,0:T(8,128)(2,1)S(1)}, u32[]{:S(2)}, u32[]{:S(2)}) collective-permute-start(bf16[64,512]{1,0:T(8,128)(2,1)S(1)} %get-tuple-element.88), channel_id=1, source_target_pairs={{224,0},{225,1},{226,2},{227,3},{228,4},{229,5},{230,6},{231,7},{2... | collective-permute-start | bytes 196616 | tf_op jit(solution)/shard_map/ppermute | solution.py:63
  37.2 8.5 %collective-permute-start.7 = (bf16[64,512]{1,0:T(8,128)(2,1)S(1)}, bf16[64,512]{1,0:T(8,128)(2,1)S(1)}, u32[]{:S(2)}, u32[]{:S(2)}) collective-permute-start(bf16[64,512]{1,0:T(8,128)(2,1)S(1)} %get-tuple-element.90), channel_id=1, source_target_pairs={{32,0},{33,1},{34,2},{35,3},{36,4},{37,5},{38,6},{39,7},{40,8},{41... | collective-permute-start | bytes 196616 | tf_op jit(solution)/shard_map/ppermute | solution.py:63
  46.1 15.9 %collective-permute-start.11 = (bf16[1024,4,128]{2,1,0:T(4,128)(2,1)S(1)}, bf16[1024,4,128]{2,1,0:T(4,128)(2,1)S(1)}, u32[]{:S(2)}, u32[]{:S(2)}) collective-permute-start(bf16[1024,4,128]{2,1,0:T(4,128)(2,1)S(1)} %constant_dynamic-update-slice_fusion.refs_13_), channel_id=1, source_target_pairs={{64,0},{65,1},{66,2},{67,3},{68,4},{69,5},{70,6},{71,7},{72,8},{73... | collective-permute-start | bytes 3145736 | tf_op jit(solution)/shard_map/ppermute | solution.py:63
  47.3 17.0 %collective-permute-start.13 = (bf16[1024,4,128]{2,1,0:T(4,128)(2,1)S(1)}, bf16[1024,4,128]{2,1,0:T(4,128)(2,1)S(1)}, u32[]{:S(2)}, u32[]{:S(2)}) collective-permute-start(bf16[1024,4,128]{2,1,0:T(4,128)(2,1)S(1)} %constant_dynamic-update-slice_fusion.refs_13_), channel_id=1, source_target_pairs={{1,0},{2,1},{3,2},{4,3},{5,4},{6,5},{7,6},{0,7},{9,8},{10,9},{11,1... | collective-permute-start | bytes 3145736 | tf_op jit(solution)/shard_map/ppermute | solution.py:63
  47.4 16.9 %collective-permute-start.12 = (bf16[1024,4,128]{2,1,0:T(4,128)(2,1)S(1)}, bf16[1024,4,128]{2,1,0:T(4,128)(2,1)S(1)}, u32[]{:S(2)}, u32[]{:S(2)}) collective-permute-start(bf16[1024,4,128]{2,1,0:T(4,128)(2,1)S(1)} %constant_dynamic-update-slice_fusion.refs_13_), channel_id=1, source_target_pairs={{8,0},{9,1},{10,2},{11,3},{12,4},{13,5},{14,6},{15,7},{16,8},{17,9... | collective-permute-start | bytes 3145736 | tf_op jit(solution)/shard_map/ppermute | solution.py:63
  47.5 17.5 %collective-permute-start.14 = (bf16[1024,4,128]{2,1,0:T(4,128)(2,1)S(1)}, bf16[1024,4,128]{2,1,0:T(4,128)(2,1)S(1)}, u32[]{:S(2)}, u32[]{:S(2)}) collective-permute-start(bf16[1024,4,128]{2,1,0:T(4,128)(2,1)S(1)} %constant_dynamic-update-slice_fusion.refs_13_), channel_id=1, source_target_pairs={{32,0},{33,1},{34,2},{35,3},{36,4},{37,5},{38,6},{39,7},{40,8},{41... | collective-permute-start | bytes 3145736 | tf_op jit(solution)/shard_map/ppermute | solution.py:63
  62.0 3.0 %collective-permute-start.15 = (bf16[1024,4,128]{2,1,0:T(4,128)(2,1)S(1)}, bf16[1024,4,128]{2,1,0:T(4,128)(2,1)S(1)}, u32[]{:S(2)}, u32[]{:S(2)}) collective-permute-start(bf16[1024,4,128]{2,1,0:T(4,128)(2,1)S(1)} %collective-permute-done.11.refs_14_), channel_id=1, source_target_pairs={{32,0},{33,1},{34,2},{35,3},{36,4},{37,5},{38,6},{39,7},{40,8},{41... | collective-permute-start | bytes 3145736 | tf_op jit(solution)/shard_map/ppermute | solution.py:63
  64.3 5.0 %collective-permute-start.16 = (bf16[1024,4,128]{2,1,0:T(4,128)(2,1)S(1)}, bf16[1024,4,128]{2,1,0:T(4,128)(2,1)S(1)}, u32[]{:S(2)}, u32[]{:S(2)}) collective-permute-start(bf16[1024,4,128]{2,1,0:T(4,128)(2,1)S(1)} %collective-permute-done.12.refs_15_), channel_id=1, source_target_pairs={{32,0},{33,1},{34,2},{35,3},{36,4},{37,5},{38,6},{39,7},{40,8},{41... | collective-permute-start | bytes 3145736 | tf_op jit(solution)/shard_map/ppermute | solution.py:63
  64.9 4.4 %collective-permute-start.17 = (bf16[1024,4,128]{2,1,0:T(4,128)(2,1)S(1)}, bf16[1024,4,128]{2,1,0:T(4,128)(2,1)S(1)}, u32[]{:S(2)}, u32[]{:S(2)}) collective-permute-start(bf16[1024,4,128]{2,1,0:T(4,128)(2,1)S(1)} %collective-permute-done.13.refs_16_), channel_id=1, source_target_pairs={{32,0},{33,1},{34,2},{35,3},{36,4},{37,5},{38,6},{39,7},{40,8},{41... | collective-permute-start | bytes 3145736 | tf_op jit(solution)/shard_map/ppermute | solution.py:63
